TPU v7x, 32 devices: a whole 2x2x4 slice. The times are simulated.
32 devices in a mesh: dp: 2 (over core), row: 4 (over y, x), col: 4 (over z).
Axes of the slice: x: 2, y: 2, z: 4, core: 2. Of those that a mesh axis runs over, the one named last changes fastest.
Arguments:
- hidden_in: bfloat16 [4096, 576], P(('dp', 'col', 'row')), may hold values from -6 to 6
- cotangent: bfloat16 [4096, 576], P(('dp', 'col', 'row'))
- lengths: int32 [8], P(('dp', 'col')), may hold values from 1 to 512, as said below
- gains: float32 [2, 2, 576], replicated, may hold values from 0.5 to 1.5
- w_qkv: bfloat16 [2, 576, 960], P(None, 'col', 'row'), may hold values from -0.25 to 0.25
- w_out: bfloat16 [2, 576, 576], P(None, 'row', 'col'), may hold values from -1.5 to 1.5
- w_gate: bfloat16 [2, 576, 1536], P(None, 'col', 'row'), may hold values from -0.25 to 0.25
- w_up: bfloat16 [2, 576, 1536], P(None, 'col', 'row'), may hold values from -0.25 to 0.25
- w_down: bfloat16 [2, 1536, 576], P(None, 'row', 'col'), may hold values from -0.15625 to 0.15625
Outputs:
- hidden_out: bfloat16 [4096, 576], P(('dp', 'col', 'row'))
- grad_hidden: float32 [4096, 576], P(('dp', 'col', 'row'))
- grad_gains: float32 [2, 2, 576], replicated
- grad_qkv: float32 [2, 576, 960], P(None, 'col', 'row')
- grad_out: float32 [2, 576, 576], P(None, 'row', 'col')
- grad_gate: float32 [2, 576, 1536], P(None, 'col', 'row')
- grad_up: float32 [2, 576, 1536], P(None, 'col', 'row')
- grad_down: float32 [2, 1536, 576], P(None, 'row', 'col')
Inputs may be any that keep to these rules, and one draw needn't show every extreme that they name: Pack p holds one sequence of lengths[p] tokens at its start; the rest of the pack is padding. Some pack holds exactly 512 tokens.
All inputs are finite; a program needn't handle non-finite values.
Results may differ from a plain program's by a relative error of at most 0.03.
Values may be sent and summed in bfloat16 or wider, within the bound.
No kernel may reach another device: no remote copies, remote signals or barrier semaphores. Data moves between devices by JAX's collectives and lax.ppermute only.
A program may use at most 128 MiB of HBM per device.

v0:
```python
import jax
import jax.numpy as jnp
from jax import lax
from jax.sharding import PartitionSpec as P

D = 576
HEADS = 9
KV_HEADS = 3
HEAD_DIM = 64
GROUP = HEADS // KV_HEADS
KV = KV_HEADS * HEAD_DIM
QKV = D + 2 * KV

eps_norm = 1e-05
rope_base = 100000.0
masked_score = -1e30
bf16 = jnp.bfloat16
f32 = jnp.float32


def mm(spec, left, right):
    return jnp.einsum(spec, left, right, preferred_element_type=f32)


def rope_tables(first_place, amount):
    half_dim = HEAD_DIM // 2
    places = (first_place + jnp.arange(amount)).astype(f32)
    frequency = rope_base ** (-(2.0 * jnp.arange(half_dim).astype(f32)) / HEAD_DIM)
    angles = places[:, None] * frequency[None, :]
    return (jnp.cos(angles)[:, None, :], jnp.sin(angles)[:, None, :])


def rotate(values, cosine, sine_vals):
    half_dim = values.shape[-1] // 2
    first_half = values[..., :half_dim]
    second_half = values[..., half_dim:]
    return jnp.concatenate(
        [
            first_half * cosine - second_half * sine_vals,
            second_half * cosine + first_half * sine_vals,
        ],
        -1,
    )


def norm_back(resid, inverse, gain, grad_norm):
    scaled = resid * inverse
    weighted = grad_norm * gain
    return inverse * (weighted - scaled * jnp.mean(weighted * scaled, -1, keepdims=True))


def swap(values, axis, bit):
    return lax.ppermute(values, axis, [(i, i ^ bit) for i in range(lax.axis_size(axis))])


def spread(values, axis):
    copies = jnp.broadcast_to(values[None], (lax.axis_size(axis),) + values.shape)
    return lax.all_to_all(copies, axis, 0, 0, tiled=True)


def scatter_sum(values, axis):
    place = lax.axis_index(axis)
    total = lax.dynamic_index_in_dim(values, place, 0, keepdims=False).astype(f32)
    for bits in range(1, lax.axis_size(axis)):
        send = lax.dynamic_index_in_dim(values, place ^ bits, 0, keepdims=False)
        total = total + swap(send, axis, bits).astype(f32)
    return total


def after(values, *earlier):
    return lax.optimization_barrier((values,) + earlier)[0]


def merge_halves(own, other, core):
    low = jnp.where(core == 0, own, other)
    high = jnp.where(core == 0, other, own)
    return jnp.stack([low, high], -3)


def sum_pairs(values):
    size = lax.axis_size("dp")
    total = values.astype(f32)
    for step in range(2, size, 2):
        moved = lax.ppermute(values, "dp", [(i, (i + step) % size) for i in range(size)])
        total = total + moved.astype(f32)
    return total.astype(values.dtype)


def halve(values, core):
    axis = values.ndim - 3
    keep = lax.dynamic_index_in_dim(values, core, axis, keepdims=False)
    send = lax.dynamic_index_in_dim(values, 1 - core, axis, keepdims=False)
    return sum_pairs((keep.astype(f32) + swap(send, "dp", 1).astype(f32)).astype(bf16))


def on_device(hidden_in, cotangent, lengths, gains, w_qkv, w_out, w_gate, w_up, w_down):
    rows = hidden_in.shape[0]
    size_row = lax.axis_size("row")
    size_col = lax.axis_size("col")
    core = lax.axis_index("dp") % 2
    first_place = lax.axis_index("row") * rows
    pack = rows * size_row
    length = lengths[0]
    layers, deep, wide_qkv = w_qkv.shape
    wide_out = w_out.shape[1]
    wide = w_gate.shape[2]
    half = deep // 2
    score_scale = HEAD_DIM ** (-0.5)

    both = wide_qkv + wide_out
    attn_blocks = jnp.concatenate([w_qkv, jnp.swapaxes(w_out, 1, 2)], -1)
    attn_half = lax.dynamic_slice_in_dim(attn_blocks, core * half, half, 1)
    feed_blocks = jnp.stack([w_gate, w_up, jnp.swapaxes(w_down, 1, 2)], 1)
    feed_half = lax.dynamic_slice_in_dim(feed_blocks, core * half, half, 2)
    full_attn, full_gate, full_up, full_down = [], [], [], []
    part = None
    for layer in range(layers):
        mine = attn_half[layer] if part is None else after(attn_half[layer], part)
        part = spread(spread(mine, "col"), "row")
        whole = merge_halves(part, swap(part, "dp", 1), core)
        full_attn.append(whole.reshape(size_row, D, both))
    feed_parts = lax.all_gather(feed_half, "col", axis=2)
    for layer in range(layers):
        part = feed_parts[layer]
        part = jnp.stack([part, swap(part, "row", 2)], 1)
        whole = merge_halves(part, swap(part, "dp", 1), core).reshape(3, 2, D, wide)
        full_gate.append(whole[0])
        full_up.append(whole[1])
        full_down.append(whole[2])

    cosine, sine_vals = rope_tables(0, pack)
    own_cosine, own_sine = rope_tables(first_place, rows)
    key_places = jnp.arange(pack)
    query_places = first_place + jnp.arange(rows)
    visible = (key_places[None, :] <= query_places[:, None]) & (key_places[None, :] < length)

    def own_rows(values):
        return lax.dynamic_slice_in_dim(values, first_place, rows, 0)

    resid = hidden_in.astype(f32)
    both_cotangent = jnp.concatenate([cotangent, swap(cotangent, "row", 1)], 0)
    stored = []
    for layer in range(layers):
        if layer == 0:
            resid_all = lax.all_gather(hidden_in, "row", axis=0, tiled=True).astype(f32)
            inverse_all = lax.rsqrt(jnp.mean(resid_all * resid_all, -1, keepdims=True) + eps_norm)
            scaled_all = resid_all * inverse_all
            normed_all = (scaled_all * gains[layer, 0]).astype(bf16)
            inverse1 = own_rows(inverse_all)
        else:
            inverse1 = lax.rsqrt(jnp.mean(resid * resid, -1, keepdims=True) + eps_norm)
            normed1 = (resid * inverse1 * gains[layer, 0]).astype(bf16)
            normed_all = lax.all_gather(normed1, "row", axis=0, tiled=True)
        mixed = mm("td,rdk->trk", normed_all, full_attn[layer])[:, :, :wide_qkv]
        mixed = mixed.astype(bf16).reshape(pack, QKV)
        query = own_rows(mixed[:, :D]).astype(f32).reshape(rows, HEADS, HEAD_DIM)
        query_rot = rotate(query, own_cosine, own_sine).astype(bf16)
        query_rot = query_rot.reshape(rows, KV_HEADS, GROUP, HEAD_DIM)
        keys = mixed[:, D : D + KV].astype(f32).reshape(pack, KV_HEADS, HEAD_DIM)
        keys_rot = rotate(keys, cosine, sine_vals).astype(bf16)
        values = mixed[:, D + KV :].reshape(pack, KV_HEADS, HEAD_DIM)
        scores = mm("qghd,kgd->ghqk", query_rot, keys_rot) * score_scale
        scores = jnp.where(visible, scores, masked_score)
        top_score = jnp.max(scores, -1, keepdims=True)
        raw_weights = jnp.exp(scores - top_score)
        probs = raw_weights / jnp.sum(raw_weights, -1, keepdims=True)
        attended = mm("ghqk,kgd->qghd", probs.astype(bf16), values)
        attended = attended.reshape(rows, D).astype(bf16)
        attended_blocks = attended.reshape(rows, size_row, wide_out)
        attended_blocks = jnp.pad(attended_blocks, ((0, 0), (0, 0), (wide_qkv, 0)))
        resid_mid = resid + mm("trk,rdk->td", attended_blocks, full_attn[layer])
        inverse2 = lax.rsqrt(jnp.mean(resid_mid * resid_mid, -1, keepdims=True) + eps_norm)
        normed2 = (resid_mid * inverse2 * gains[layer, 1]).astype(bf16)
        both_normed2 = jnp.concatenate([normed2, swap(normed2, "row", 1)], 0)
        gate_act = mm("td,bdf->tbf", both_normed2, full_gate[layer])
        up_act = mm("td,bdf->tbf", both_normed2, full_up[layer])
        hidden = (gate_act * jax.nn.sigmoid(gate_act) * up_act).astype(bf16)
        down_part = mm("tbf,bdf->td", hidden, full_down[layer])
        moved = swap(down_part[rows:].astype(bf16), "row", 1).astype(f32)
        resid_next = resid_mid + down_part[:rows] + moved
        stored.append(
            (
                resid,
                inverse1,
                normed_all,
                query_rot,
                keys_rot,
                values,
                probs,
                attended_blocks,
                resid_mid,
                inverse2,
                both_normed2,
                gate_act,
                up_act,
                hidden,
            )
        )
        resid = resid_next

    grad_resid = cotangent.astype(f32)
    attn_grads = [None] * layers
    feed_grads = [None] * layers
    gain_grads = [None] * layers
    waiting = {}
    for layer in reversed(range(layers)):
        (
            resid_in,
            inverse1,
            normed_all,
            query_rot,
            keys_rot,
            values,
            probs,
            attended_blocks,
            resid_mid,
            inverse2,
            both_normed2,
            gate_act,
            up_act,
            hidden,
        ) = stored[layer]
        if layer == layers - 1:
            both_grad = both_cotangent
        else:
            grad_low = grad_resid.astype(bf16)
            both_grad = jnp.concatenate([grad_low, swap(grad_low, "row", 1)], 0)
            both_grad = after(both_grad, waiting["feed_two"])
        grad_hid = mm("td,bdf->tbf", both_grad, full_down[layer])
        sigma = jax.nn.sigmoid(gate_act)
        grad_gate_act = (grad_hid * up_act * sigma * (1.0 + gate_act * (1.0 - sigma))).astype(bf16)
        grad_up_act = (grad_hid * gate_act * sigma).astype(bf16)
        norm2_part = mm("tbf,bdf->td", grad_gate_act, full_gate[layer])
        norm2_part = norm2_part + mm("tbf,bdf->td", grad_up_act, full_up[layer])
        moved = norm2_part[rows:].astype(bf16)
        if waiting:
            moved = after(moved, waiting["attn_half"])
        moved = swap(moved, "row", 1).astype(f32)
        grad_norm2 = norm2_part[:rows] + moved
        feed_grad = jnp.stack(
            [
                mm("td,tbf->bdf", both_normed2, grad_gate_act).astype(bf16),
                mm("td,tbf->bdf", both_normed2, grad_up_act).astype(bf16),
                mm("td,tbf->bdf", both_grad, hidden).astype(bf16),
            ],
            1,
        )
        feed_half_sum = halve(feed_grad.reshape(2, 3, size_col, 2, half, wide), core)
        feed_two = feed_half_sum[0].astype(f32) + swap(feed_half_sum[1], "row", 2).astype(f32)
        feed_two = jnp.swapaxes(feed_two.astype(bf16), 0, 1)
        feed_grad = scatter_sum(feed_two, "col")
        other = swap(feed_grad, "dp", 1)
        feed_grads[layer] = merge_halves(feed_grad, other, core).reshape(3, deep, wide)

        gain_grad2 = jnp.sum(grad_norm2 * (resid_mid * inverse2), 0)
        grad_resid = grad_resid + norm_back(resid_mid, inverse2, gains[layer, 1], grad_norm2)
        grad_low = grad_resid.astype(bf16)
        if waiting:
            grad_low = after(grad_low, waiting["feed_grad"])
        grad_att = mm("td,rdk->trk", grad_low, full_attn[layer])[:, :, wide_qkv:].astype(bf16)
        grad_att = grad_att.reshape(rows, KV_HEADS, GROUP, HEAD_DIM)
        grad_out = mm("td,trk->rdk", grad_low, attended_blocks)
        grad_probs = mm("qghd,kgd->ghqk", grad_att, values)
        row_dots = jnp.sum(grad_probs * probs, -1, keepdims=True)
        grad_scores = (probs * (grad_probs - row_dots)).astype(bf16)
        grad_query = mm("ghqk,kgd->qghd", grad_scores, keys_rot) * score_scale
        grad_keys = mm("ghqk,qghd->kgd", grad_scores, query_rot) * score_scale
        grad_values = mm("ghqk,qghd->kgd", probs.astype(bf16), grad_att)
        grad_query = rotate(grad_query.reshape(rows, HEADS, HEAD_DIM), own_cosine, -own_sine)
        grad_keys = rotate(grad_keys, cosine, -sine_vals)
        grad_query = grad_query.reshape(rows, D).astype(bf16)
        grad_query = lax.dynamic_update_slice_in_dim(
            jnp.zeros((pack, D), bf16), grad_query, first_place, 0
        )
        grad_mixed = jnp.concatenate(
            [
                grad_query,
                grad_keys.reshape(pack, KV).astype(bf16),
                grad_values.reshape(pack, KV).astype(bf16),
            ],
            -1,
        ).reshape(pack, size_row, wide_qkv)
        grad_mixed = jnp.pad(grad_mixed, ((0, 0), (0, 0), (0, wide_out)))
        grad_mixed = after(grad_mixed, feed_half_sum)
        if waiting:
            grad_mixed = after(grad_mixed, waiting["attn_row"])
        norm1_part = mm("trk,rdk->td", grad_mixed, full_attn[layer])
        norm1_blocks = norm1_part.astype(bf16).reshape(size_row, rows, D)
        if layer == 0:
            grad_norm1 = scatter_sum(norm1_blocks, "row")
        else:
            grad_norm1 = lax.all_to_all(norm1_blocks, "row", 0, 0, tiled=True)
            grad_norm1 = jnp.sum(grad_norm1.astype(f32), 0)
        if layer == 0:
            gain_grad1 = jnp.sum(norm1_part * scaled_all, 0)
        else:
            gain_grad1 = jnp.sum(grad_norm1 * (resid_in * inverse1), 0)
        grad_resid = grad_resid + norm_back(resid_in, inverse1, gains[layer, 0], grad_norm1)
        gain_grads[layer] = jnp.stack([gain_grad1, gain_grad2], 0)
        attn_grad = (mm("td,trk->rdk", normed_all, grad_mixed) + grad_out).astype(bf16)
        attn_grad = halve(attn_grad.reshape(size_row, size_col, 2, half, both), core)
        if layer == 0:
            gain_part = jnp.stack(gain_grads, 0)
            gain_part = sum_pairs((gain_part + swap(gain_part, "dp", 1)).astype(bf16))
            gain_rows = gain_part.reshape(-1, both)
            extra = gain_rows.shape[0]
            gain_rows = jnp.pad(gain_rows, ((0, -extra % 8), (0, 0)))
            gain_rows = jnp.broadcast_to(gain_rows, (size_row, size_col) + gain_rows.shape)
            attn_grad = jnp.concatenate([attn_grad, gain_rows], 2)
        waiting = {"feed_two": feed_two, "feed_grad": feed_grad, "attn_half": attn_grad}
        attn_grad = lax.all_to_all(attn_grad, "row", 0, 0, tiled=True)
        attn_grad = jnp.sum(attn_grad.astype(f32), 0).astype(bf16)
        waiting["attn_row"] = attn_grad
        attn_grad = lax.all_to_all(attn_grad, "col", 0, 0, tiled=True)
        attn_grad = jnp.sum(attn_grad.astype(f32), 0)
        if layer == 0:
            gain_total = attn_grad[half : half + extra].reshape(layers, 2, D)
            attn_grad = attn_grad[:half]
        other = swap(attn_grad, "dp", 1)
        attn_grads[layer] = merge_halves(attn_grad, other, core).reshape(deep, -1)

    attn_grads = jnp.stack(attn_grads, 0)
    feed_grads = jnp.stack(feed_grads, 0)
    return (
        resid.astype(bf16),
        grad_resid,
        gain_total,
        attn_grads[:, :, :wide_qkv],
        jnp.swapaxes(attn_grads[:, :, wide_qkv:], 1, 2),
        feed_grads[:, 0],
        feed_grads[:, 1],
        jnp.swapaxes(feed_grads[:, 2], 1, 2),
    )


def solution(mesh):
    tokens = P(("dp", "col", "row"), None)
    return jax.shard_map(
        on_device,
        mesh=mesh,
        in_specs=(
            tokens,
            tokens,
            P(("dp", "col")),
            P(),
            P(None, "col", "row"),
            P(None, "row", "col"),
            P(None, "col", "row"),
            P(None, "col", "row"),
            P(None, "row", "col"),
        ),
        out_specs=(
            tokens,
            tokens,
            P(),
            P(None, "col", "row"),
            P(None, "row", "col"),
            P(None, "col", "row"),
            P(None, "col", "row"),
            P(None, "row", "col"),
        ),
        check_vma=False,
    )
```

profile of v0, /device:TPU:1, one launch (start us, length us, event | category | flops | bytes accessed | tf_op | source)
XLA Modules:
  0.0 354.1 jit_solution(891539803542915008)
XLA Ops:
  10.1 5.4 %all-to-all-start = ((bf16[4,72,384]{2,1,0:T(8,128)(2,1)}), bf16[4,72,384]{2,1,0:T(8,128)(2,1)S(1)}, u32[]{:S(2)}, u32[]{:S(2)}) async-start(bf16[4,72,384]{2,1,0:T(8,128)(2,1)} %broadcast_in_dim.21), calls=%async_computation | async-start | bytes 442368 | tf_op jit(solution)/shard_map/all_to_all | solution.py:58
  18.2 2.7 all-to-all-done
  21.9 3.5 all-to-all-start.1
  25.5 15.6 %all_gather.12 = bf16[512,576]{0,1:T(8,128)(2,1)S(1)} all-gather(bf16[128,576]{0,1:T(8,128)(2,1)S(1)} %copy-done.40), channel_id=1, replica_groups=mesh['dp'=2,'row'=4,'col'=4] {'row'}, dimensions={0}, use_global_device_ids=true | all-gather | bytes 737280 | tf_op jit(solution)/shard_map/all_gather | solution.py:145
  42.7 5.0 %collective-permute-start = (bf16[4,4,72,384]{3,2,1,0:T(8,128)(2,1)S(1)}, bf16[4,4,72,384]{3,2,1,0:T(8,128)(2,1)S(1)}, u32[]{:S(2)}, u32[]{:S(2)}) collective-permute-start(bf16[4,4,72,384]{3,2,1,0:T(8,128)(2,1)S(1)} %all-to-all-done.1), channel_id=1, source_target_pairs={{0,16},{16,0},{1,17},{17,1},{2,18},{18,2},{3,19},{19,3},{4,20},{20... | collective-permute-start | bytes 2654216 | tf_op jit(solution)/shard_map/ppermute | solution.py:53
  49.2 3.4 all-to-all-start.2
  53.6 5.7 %all-to-all-done.2 = bf16[4,72,384]{2,1,0:T(8,128)(2,1)S(1)} async-done(((bf16[4,72,384]{2,1,0:T(8,128)(2,1)}), bf16[4,72,384]{2,1,0:T(8,128)(2,1)S(1)}, u32[]{:S(2)}, u32[]{:S(2)}) %all-to-all-start.2) | async-done | bytes 221216 | tf_op jit(solution)/shard_map/all_to_all | solution.py:58
  60.2 4.4 %all-to-all-start.3 = ((bf16[4,4,72,384]{3,2,1,0:T(8,128)(2,1)}), bf16[4,4,72,384]{3,2,1,0:T(8,128)(2,1)}, u32[]{:S(2)}, u32[]{:S(2)}) async-start(bf16[4,4,72,384]{3,2,1,0:T(8,128)(2,1)} %broadcast_in_dim.26), calls=%async_computation.3 | async-start | bytes 1769472 | tf_op jit(solution)/shard_map/all_to_all | solution.py:58
  65.0 1.5 fusion.71
  68.3 1.5 fusion.135
  69.8 1.5 collective-permute-start.2
  72.1 3.3 fusion.138
  75.4 2.8 convolution_convert_fusion.7
  79.3 2.9 collective-permute-start.5
  82.2 8.0 %collective-permute-done.2 = bf16[3,4,72,384]{3,2,1,0:T(8,128)(2,1)} collective-permute-done((bf16[3,4,72,384]{3,2,1,0:T(8,128)(2,1)S(1)}, bf16[3,4,72,384]{3,2,1,0:T(8,128)(2,1)}, u32[]{:S(2)}, u32[]{:S(2)}) %collective-permute-start.2) | collective-permute-done | bytes 663584 | tf_op jit(solution)/shard_map/ppermute | solution.py:53
  91.5 2.5 collective-permute-start.3
  96.3 8.1 %collective-permute-done.7 = bf16[3,4,72,384]{3,2,1,0:T(8,128)(2,1)S(1)} collective-permute-done((bf16[3,4,72,384]{3,2,1,0:T(8,128)(2,1)S(1)}, bf16[3,4,72,384]{3,2,1,0:T(8,128)(2,1)S(1)}, u32[]{:S(2)}, u32[]{:S(2)}) %collective-permute-start.7) | collective-permute-done | bytes 663584 | tf_op jit(solution)/shard_map/ppermute | solution.py:53
  104.5 1.5 collective-permute-start.8
  112.2 1.5 multiply_convert_fusion.5
  120.7 8.5 %all_gather.15 = bf16[512,576]{0,1:T(8,128)(2,1)S(1)} all-gather(bf16[128,576]{0,1:T(8,128)(2,1)S(1)} %multiply_convert_fusion.7), channel_id=1, replica_groups=mesh['dp'=2,'row'=4,'col'=4] {'row'}, dimensions={0}, use_global_device_ids=true | all-gather | bytes 737280 | tf_op jit(solution)/shard_map/all_gather | solution.py:153
  129.1 1.4 fusion.45
  133.0 3.9 %fusion.139 = (f32[3,3,128]{2,1,0:T(4,128)}, f32[3,3,128,512]{2,3,1,0:T(8,128)}) fusion(pred[128,512]{0,1:T(8,128)(4,1)} %copy-done.91, bf16[512,3,32]{0,2,1:T(8,128)(2,1)} %get-tuple-element.127, bf16[512,3,32]{0,2,1:T(8,128)(2,1)} %get-tuple-element.126, bf16[128,3,3,32]{0,3,2,1:T(8,128)(2,1)} %bitcast.555, bf16[128,3,3,32]{0,3,2,1:T(8,128)(2,1)} %bitcast.551), kind=kOutput, calls=%fused_computation.355 | convolution fusion | flops 78545408 | bytes 2773504 | tf_op jit(solution)/shard_map/sub | solution.py:165
  136.9 2.9 convolution_convert_fusion.6
  139.9 1.7 copy.148
  141.6 1.8 multiply_reduce_fusion.6
  144.0 1.6 fusion.93
  145.6 2.1 collective-permute-done.6
  155.8 4.6 %collective-permute-start.12 = (bf16[2,3,4,72,384]{4,3,2,0,1:T(8,128)(2,1)}, bf16[2,3,4,72,384]{4,3,2,0,1:T(8,128)(2,1)}, u32[]{:S(2)}, u32[]{:S(2)}) collective-permute-start(bf16[2,3,4,72,384]{4,3,2,0,1:T(8,128)(2,1)} %dynamic-slice_bitcast_fusion), channel_id=1, source_target_pairs={{0,16},{16,0},{1,17},{17,1},{2,18},{18,2},{3,19},{19,3},{4,20},{20... | collective-permute-start | bytes 3981320 | tf_op jit(solution)/shard_map/ppermute | solution.py:53
  160.7 1.7 multiply_add_fusion.2
  169.6 3.4 fusion.35
  175.4 2.4 fusion.56
  179.0 2.8 fusion.3
  183.8 4.1 %all-to-all-start.4 = ((bf16[4,128,576]{1,2,0:T(8,128)(2,1)}), bf16[4,128,576]{1,2,0:T(8,128)(2,1)}, u32[]{:S(2)}, u32[]{:S(2)}) async-start(bf16[4,128,576]{1,2,0:T(8,128)(2,1)} %bitcast.528), calls=%async_computation.4 | async-start | bytes 1179648 | tf_op jit(solution)/shard_map/all_to_all | solution.py:292
  188.9 5.1 %add_convert_fusion.1 = bf16[4,384,576]{1,2,0:T(8,128)(2,1)} fusion(f32[4,384,576]{1,2,0:T(8,128)} %fusion.56, bf16[512,4,384]{0,2,1:T(8,128)(2,1)} %copy-done.11, bf16[512,576]{0,1:T(8,128)(2,1)} %copy-done.32), kind=kOutput, calls=%fused_computation.3 | convolution fusion | flops 907739136 | bytes 7471104 | tf_op jit(solution)/shard_map/td,trk->rdk/dot_general | solution.py:22
  194.0 3.0 all-to-all-done.4
  198.6 1.9 fusion.133
  212.5 1.6 collective-permute-start.20
  214.1 5.2 %collective-permute-done.16 = bf16[3,4,72,384]{3,2,1,0:T(8,128)(2,1)S(1)} collective-permute-done((bf16[3,4,72,384]{3,2,1,0:T(8,128)(2,1)S(1)}, bf16[3,4,72,384]{3,2,1,0:T(8,128)(2,1)S(1)}, u32[]{:S(2)}, u32[]{:S(2)}) %collective-permute-start.16) | collective-permute-done | bytes 663584 | tf_op jit(solution)/shard_map/ppermute | solution.py:53
  219.6 2.3 collective-permute-start.19
  224.8 1.6 collective-permute-done.19
  226.5 9.4 %collective-permute-done.18 = bf16[3,72,384]{2,1,0:T(8,128)(2,1)S(1)} collective-permute-done((bf16[3,72,384]{2,1,0:T(8,128)(2,1)S(1)}, bf16[3,72,384]{2,1,0:T(8,128)(2,1)S(1)}, u32[]{:S(2)}, u32[]{:S(2)}) %collective-permute-start.18) | collective-permute-done | bytes 165920 | tf_op jit(solution)/shard_map/ppermute | solution.py:53
  236.7 1.7 collective-permute-start.33
  238.4 4.4 %all-to-all-start.5 = ((bf16[4,4,72,384]{3,2,1,0:T(8,128)(2,1)}), bf16[4,4,72,384]{3,2,1,0:T(8,128)(2,1)}, u32[]{:S(2)}, u32[]{:S(2)}) async-start(bf16[4,4,72,384]{3,2,1,0:T(8,128)(2,1)} %fusion.13), calls=%async_computation.5 | async-start | bytes 1769472 | tf_op jit(solution)/shard_map/all_to_all | solution.py:311
  243.2 1.7 fusion.132
  249.5 2.0 fusion.36
  251.8 3.1 all-to-all-done.5
  254.9 2.0 reduce_sum.207
  256.9 4.0 %all-to-all-start.8 = ((bf16[4,72,384]{2,1,0:T(8,128)(2,1)}), bf16[4,72,384]{2,1,0:T(8,128)(2,1)}, u32[]{:S(2)}, u32[]{:S(2)}) async-start(bf16[4,72,384]{2,1,0:T(8,128)(2,1)} %reduce_sum.207), calls=%async_computation.8 | async-start | bytes 442368 | tf_op jit(solution)/shard_map/all_to_all | solution.py:314
  263.1 3.5 all-to-all-done.8
  266.5 1.6 convert_reduce_fusion.2
  268.1 3.5 collective-permute-start.27
  271.6 2.1 fusion.2
  273.8 1.9 fusion.27
  275.8 2.9 fusion.69
  285.4 2.6 add_convert_fusion
  293.4 12.6 %collective-permute-done.28 = bf16[3,4,72,384]{3,2,0,1:T(8,128)(2,1)} collective-permute-done((bf16[3,4,72,384]{3,2,0,1:T(8,128)(2,1)}, bf16[3,4,72,384]{3,2,0,1:T(8,128)(2,1)}, u32[]{:S(2)}, u32[]{:S(2)}) %collective-permute-start.28) | collective-permute-done | bytes 663584 | tf_op jit(solution)/shard_map/ppermute | solution.py:53
  310.2 2.4 collective-permute-start.29
  313.7 3.6 %all-to-all-start.6 = ((bf16[4,4,80,384]{3,2,1,0:T(8,128)(2,1)}), bf16[4,4,80,384]{3,2,1,0:T(8,128)(2,1)S(1)}, u32[]{:S(2)}, u32[]{:S(2)}) async-start(bf16[4,4,80,384]{3,2,1,0:T(8,128)(2,1)} %pad_maximum_fusion.8), calls=%async_computation.6 | async-start | bytes 1966080 | tf_op jit(solution)/shard_map/all_to_all | solution.py:311
  318.5 4.8 %collective-permute-done.30 = bf16[3,72,384]{2,1,0:T(8,128)(2,1)S(1)} collective-permute-done((bf16[3,72,384]{2,1,0:T(8,128)(2,1)S(1)}, bf16[3,72,384]{2,1,0:T(8,128)(2,1)S(1)}, u32[]{:S(2)}, u32[]{:S(2)}) %collective-permute-start.30) | collective-permute-done | bytes 165920 | tf_op jit(solution)/shard_map/ppermute | solution.py:53
  325.7 1.9 fusion.76
  327.5 2.1 all-to-all-done.6
  330.5 3.4 all-to-all-start.7
  334.1 5.4 %all-to-all-done.7 = bf16[4,80,384]{2,1,0:T(8,128)(2,1)S(1)} async-done(((bf16[4,80,384]{2,1,0:T(8,128)(2,1)}), bf16[4,80,384]{2,1,0:T(8,128)(2,1)S(1)}, u32[]{:S(2)}, u32[]{:S(2)}) %all-to-all-start.7) | async-done | bytes 245792 | tf_op jit(solution)/shard_map/all_to_all | solution.py:314
  339.5 3.9 %collective-permute-start.26 = (f32[72,384]{1,0:T(8,128)S(1)}, f32[72,384]{1,0:T(8,128)S(1)}, u32[]{:S(2)}, u32[]{:S(2)}) collective-permute-start(f32[72,384]{1,0:T(8,128)S(1)} %slice.305), channel_id=1, source_target_pairs={{0,16},{16,0},{1,17},{17,1},{2,18},{18,2},{3,19},{19,3},{4,20},{20... | collective-permute-start | bytes 331784 | tf_op jit(solution)/shard_map/ppermute | solution.py:53
  (436 shorter events, 106.0 us)
Async XLA Ops:
  10.1 10.9 %all-to-all-start = ((bf16[4,72,384]{2,1,0:T(8,128)(2,1)}), bf16[4,72,384]{2,1,0:T(8,128)(2,1)S(1)}, u32[]{:S(2)}, u32[]{:S(2)}) async-start(bf16[4,72,384]{2,1,0:T(8,128)(2,1)} %broadcast_in_dim.21), calls=%async_computation | async-start | bytes 442368 | tf_op jit(solution)/shard_map/all_to_all | solution.py:58
  15.5 52.8 %all-gather.3.cloned.1.call-start = ((), (), s32[]{:S(2)}) async-start(), calls=%async_computation.9 | async-start | bytes 1658880 | tf_op jit(solution)/shard_map/all_gather | solution.py:122
  16.3 127.7 %collective-permute-start.10 = (bf16[128,576]{0,1:T(8,128)(2,1)}, bf16[128,576]{0,1:T(8,128)(2,1)}, u32[]{:S(2)}, u32[]{:S(2)}) collective-permute-start(bf16[128,576]{0,1:T(8,128)(2,1)} %param.10), channel_id=1, source_target_pairs={{0,4},{4,0},{8,12},{12,8},{1,5},{5,1},{9,13},{13,9},{2,6},{6,2},{1... | collective-permute-start | bytes 442376 | tf_op jit(solution)/shard_map/ppermute | solution.py:53
  18.2 22.9 %copy-start.94 = (f32[2,2,576]{2,1,0:T(2,128)S(1)}, f32[2,2,576]{2,1,0:T(2,128)}, u32[]{:S(2)}) copy-start(f32[2,2,576]{2,1,0:T(2,128)} %param.12) | copy-start | bytes 27652
  21.9 20.8 %all-to-all-start.1 = ((bf16[4,4,72,384]{3,2,1,0:T(8,128)(2,1)}), bf16[4,4,72,384]{3,2,1,0:T(8,128)(2,1)S(1)}, u32[]{:S(2)}, u32[]{:S(2)}) async-start(bf16[4,4,72,384]{3,2,1,0:T(8,128)(2,1)} %broadcast_in_dim.22), calls=%async_computation.1 | async-start | bytes 1769472 | tf_op jit(solution)/shard_map/all_to_all | solution.py:58
  41.1 23.9 %copy-start.16 = (bf16[512,576]{0,1:T(8,128)(2,1)}, bf16[512,576]{0,1:T(8,128)(2,1)S(1)}, u32[]{:S(2)}) copy-start(bf16[512,576]{0,1:T(8,128)(2,1)S(1)} %all_gather.12) | copy-start | bytes 1769476
  41.8 23.2 %copy-start.84 = (f32[576]{0:T(1024)}, f32[576]{0:T(1024)S(1)}, u32[]{:S(2)}) copy-start(f32[576]{0:T(1024)S(1)} %get-tuple-element.68) | copy-start | bytes 6916
  41.8 53.0 %copy-start.86 = (f32[576]{0:T(1024)}, f32[576]{0:T(1024)S(1)}, u32[]{:S(2)}) copy-start(f32[576]{0:T(1024)S(1)} %get-tuple-element.67) | copy-start | bytes 6916
  42.7 28.6 %copy-start.82 = (f32[128,32]{0,1:T(8,128)}, f32[128,32]{0,1:T(8,128)S(1)}, u32[]{:S(2)}) copy-start(f32[128,32]{0,1:T(8,128)S(1)} %get-tuple-element.150) | copy-start | bytes 49156
  42.7 21.9 %collective-permute-start = (bf16[4,4,72,384]{3,2,1,0:T(8,128)(2,1)S(1)}, bf16[4,4,72,384]{3,2,1,0:T(8,128)(2,1)S(1)}, u32[]{:S(2)}, u32[]{:S(2)}) collective-permute-start(bf16[4,4,72,384]{3,2,1,0:T(8,128)(2,1)S(1)} %all-to-all-done.1), channel_id=1, source_target_pairs={{0,16},{16,0},{1,17},{17,1},{2,18},{18,2},{3,19},{19,3},{4,20},{20... | collective-permute-start | bytes 2654216 | tf_op jit(solution)/shard_map/ppermute | solution.py:53
  47.7 17.4 %copy-start.95 = (f32[512]{0:T(512)}, f32[512]{0:T(512)S(1)}, u32[]{:S(2)}) copy-start(f32[512]{0:T(512)S(1)} %add_rsqrt_fusion) | copy-start | bytes 6148
  48.5 26.9 %copy-start.91 = (pred[128,512]{0,1:T(8,128)(4,1)}, pred[128,512]{0,1:T(8,128)(4,1)S(1)}, u32[]{:S(2)}) copy-start(pred[128,512]{0,1:T(8,128)(4,1)S(1)} %fusion.88) | copy-start | bytes 196612
  49.2 10.1 %all-to-all-start.2 = ((bf16[4,72,384]{2,1,0:T(8,128)(2,1)}), bf16[4,72,384]{2,1,0:T(8,128)(2,1)S(1)}, u32[]{:S(2)}, u32[]{:S(2)}) async-start(bf16[4,72,384]{2,1,0:T(8,128)(2,1)} %broadcast_in_dim.25), calls=%async_computation.2 | async-start | bytes 442368 | tf_op jit(solution)/shard_map/all_to_all | solution.py:58
  53.6 14.6 %copy-start.43 = (f32[512,32]{0,1:T(8,128)}, f32[512,32]{0,1:T(8,128)S(1)}, u32[]{:S(2)}) copy-start(f32[512,32]{0,1:T(8,128)S(1)} %get-tuple-element.148) | copy-start | bytes 196612
  53.6 14.6 %copy-start.60 = (f32[512,32]{0,1:T(8,128)}, f32[512,32]{0,1:T(8,128)S(1)}, u32[]{:S(2)}) copy-start(f32[512,32]{0,1:T(8,128)S(1)} %get-tuple-element.147) | copy-start | bytes 196612
  60.2 19.0 %all-to-all-start.3 = ((bf16[4,4,72,384]{3,2,1,0:T(8,128)(2,1)}), bf16[4,4,72,384]{3,2,1,0:T(8,128)(2,1)}, u32[]{:S(2)}, u32[]{:S(2)}) async-start(bf16[4,4,72,384]{3,2,1,0:T(8,128)(2,1)} %broadcast_in_dim.26), calls=%async_computation.3 | async-start | bytes 1769472 | tf_op jit(solution)/shard_map/all_to_all | solution.py:58
  69.8 20.4 %copy-start.14 = (bf16[1,3,288,384]{3,2,0,1:T(8,128)(2,1)}, bf16[1,3,288,384]{3,2,0,1:T(8,128)(2,1)S(1)}, u32[]{:S(2)}) copy-start(bf16[1,3,288,384]{3,2,0,1:T(8,128)(2,1)S(1)} %get-tuple-element.101) | copy-start | bytes 1990660
  69.8 34.5 %copy-start.12 = (bf16[1,3,288,384]{3,2,0,1:T(8,128)(2,1)}, bf16[1,3,288,384]{3,2,0,1:T(8,128)(2,1)S(1)}, u32[]{:S(2)}) copy-start(bf16[1,3,288,384]{3,2,0,1:T(8,128)(2,1)S(1)} %get-tuple-element.100) | copy-start | bytes 1990660
  69.8 20.4 %collective-permute-start.2 = (bf16[3,4,72,384]{3,2,1,0:T(8,128)(2,1)S(1)}, bf16[3,4,72,384]{3,2,1,0:T(8,128)(2,1)}, u32[]{:S(2)}, u32[]{:S(2)}) collective-permute-start(bf16[3,4,72,384]{3,2,1,0:T(8,128)(2,1)S(1)} %bitcast.503), channel_id=1, source_target_pairs={{0,8},{4,12},{8,0},{12,4},{1,9},{5,13},{9,1},{13,5},{2,10},{6,14},... | collective-permute-start | bytes 1990664 | tf_op jit(solution)/shard_map/ppermute | solution.py:53
  79.3 15.5 %copy-start.37 = (bf16[128,4,144]{2,0,1:T(8,128)(2,1)}, bf16[128,4,144]{2,0,1:T(8,128)(2,1)S(1)}, u32[]{:S(2)}) copy-start(bf16[128,4,144]{2,0,1:T(8,128)(2,1)S(1)} %copy.143) | copy-start | bytes 442372
  79.3 26.8 %collective-permute-start.5 = (bf16[4,4,72,384]{3,2,1,0:T(8,128)(2,1)}, bf16[4,4,72,384]{3,2,1,0:T(8,128)(2,1)S(1)}, u32[]{:S(2)}, u32[]{:S(2)}) collective-permute-start(bf16[4,4,72,384]{3,2,1,0:T(8,128)(2,1)} %all-to-all-done.3), channel_id=1, source_target_pairs={{0,16},{16,0},{1,17},{17,1},{2,18},{18,2},{3,19},{19,3},{4,20},{20... | collective-permute-start | bytes 2654216 | tf_op jit(solution)/shard_map/ppermute | solution.py:53
  82.2 22.1 %collective-permute-start.7 = (bf16[3,4,72,384]{3,2,1,0:T(8,128)(2,1)S(1)}, bf16[3,4,72,384]{3,2,1,0:T(8,128)(2,1)S(1)}, u32[]{:S(2)}, u32[]{:S(2)}) collective-permute-start(bf16[3,4,72,384]{3,2,1,0:T(8,128)(2,1)S(1)} %bitcast.500), channel_id=1, source_target_pairs={{0,8},{4,12},{8,0},{12,4},{1,9},{5,13},{9,1},{13,5},{2,10},{6,14},... | collective-permute-start | bytes 1990664 | tf_op jit(solution)/shard_map/ppermute | solution.py:53
  91.5 16.3 %collective-permute-start.3 = (bf16[3,2,4,72,384]{4,3,2,1,0:T(8,128)(2,1)S(1)}, bf16[3,2,4,72,384]{4,3,2,1,0:T(8,128)(2,1)S(1)}, u32[]{:S(2)}, u32[]{:S(2)}) collective-permute-start(bf16[3,2,4,72,384]{4,3,2,1,0:T(8,128)(2,1)S(1)} %pad_maximum_fusion.4), channel_id=1, source_target_pairs={{0,16},{16,0},{1,17},{17,1},{2,18},{18,2},{3,19},{19,3},{4,20},{20... | collective-permute-start | bytes 3981320 | tf_op jit(solution)/shard_map/ppermute | solution.py:53
  94.8 24.9 %copy-start.6 = (f32[128,576]{0,1:T(8,128)}, f32[128,576]{0,1:T(8,128)S(1)}, u32[]{:S(2)}) copy-start(f32[128,576]{0,1:T(8,128)S(1)} %get-tuple-element.155) | copy-start | bytes 884740
  95.0 16.0 %copy-start.35 = (bf16[128,576]{0,1:T(8,128)(2,1)}, bf16[128,576]{0,1:T(8,128)(2,1)S(1)}, u32[]{:S(2)}) copy-start(bf16[128,576]{0,1:T(8,128)(2,1)S(1)} %multiply_convert_fusion.8) | copy-start | bytes 442372
  95.0 15.5 %collective-permute-start.1 = (bf16[128,576]{0,1:T(8,128)(2,1)S(1)}, bf16[128,576]{0,1:T(8,128)(2,1)S(1)}, u32[]{:S(2)}, u32[]{:S(2)}) collective-permute-start(bf16[128,576]{0,1:T(8,128)(2,1)S(1)} %multiply_convert_fusion.8), channel_id=1, source_target_pairs={{0,4},{4,0},{8,12},{12,8},{1,5},{5,1},{9,13},{13,9},{2,6},{6,2},{1... | collective-permute-start | bytes 442376 | tf_op jit(solution)/shard_map/ppermute | solution.py:53
  104.5 10.9 %collective-permute-start.8 = (bf16[3,2,4,72,384]{4,3,2,1,0:T(8,128)(2,1)S(1)}, bf16[3,2,4,72,384]{4,3,2,1,0:T(8,128)(2,1)S(1)}, u32[]{:S(2)}, u32[]{:S(2)}) collective-permute-start(bf16[3,2,4,72,384]{4,3,2,1,0:T(8,128)(2,1)S(1)} %pad_maximum_fusion.5), channel_id=1, source_target_pairs={{0,16},{16,0},{1,17},{17,1},{2,18},{18,2},{3,19},{19,3},{4,20},{20... | collective-permute-start | bytes 3981320 | tf_op jit(solution)/shard_map/ppermute | solution.py:53
  114.2 5.5 %collective-permute-start.4 = (bf16[128,576]{0,1:T(8,128)(2,1)S(1)}, bf16[128,576]{0,1:T(8,128)(2,1)S(1)}, u32[]{:S(2)}, u32[]{:S(2)}) collective-permute-start(bf16[128,576]{0,1:T(8,128)(2,1)S(1)} %slice.445), channel_id=1, source_target_pairs={{0,4},{4,0},{8,12},{12,8},{1,5},{5,1},{9,13},{13,9},{2,6},{6,2},{1... | collective-permute-start | bytes 442376 | tf_op jit(solution)/shard_map/ppermute | solution.py:53
  143.6 4.1 %collective-permute-start.6 = (bf16[128,576]{0,1:T(8,128)(2,1)S(1)}, bf16[128,576]{0,1:T(8,128)(2,1)S(1)}, u32[]{:S(2)}, u32[]{:S(2)}) collective-permute-start(bf16[128,576]{0,1:T(8,128)(2,1)S(1)} %multiply_convert_fusion.6), channel_id=1, source_target_pairs={{0,4},{4,0},{8,12},{12,8},{1,5},{5,1},{9,13},{13,9},{2,6},{6,2},{1... | collective-permute-start | bytes 442376 | tf_op jit(solution)/shard_map/ppermute | solution.py:53
  149.9 10.5 %collective-permute-start.11 = (bf16[128,576]{0,1:T(8,128)(2,1)S(1)}, bf16[128,576]{0,1:T(8,128)(2,1)S(1)}, u32[]{:S(2)}, u32[]{:S(2)}) collective-permute-start(bf16[128,576]{0,1:T(8,128)(2,1)S(1)} %slice.443), channel_id=1, source_target_pairs={{0,4},{4,0},{8,12},{12,8},{1,5},{5,1},{9,13},{13,9},{2,6},{6,2},{1... | collective-permute-start | bytes 442376 | tf_op jit(solution)/shard_map/ppermute | solution.py:53
  150.8 10.0 %collective-permute-start.9 = (bf16[128,576]{0,1:T(8,128)(2,1)S(1)}, bf16[128,576]{0,1:T(8,128)(2,1)S(1)}, u32[]{:S(2)}, u32[]{:S(2)}) collective-permute-start(bf16[128,576]{0,1:T(8,128)(2,1)S(1)} %slice.444), channel_id=1, source_target_pairs={{0,4},{4,0},{8,12},{12,8},{1,5},{5,1},{9,13},{13,9},{2,6},{6,2},{1... | collective-permute-start | bytes 442376 | tf_op jit(solution)/shard_map/ppermute | solution.py:53
  155.8 22.0 %collective-permute-start.12 = (bf16[2,3,4,72,384]{4,3,2,0,1:T(8,128)(2,1)}, bf16[2,3,4,72,384]{4,3,2,0,1:T(8,128)(2,1)}, u32[]{:S(2)}, u32[]{:S(2)}) collective-permute-start(bf16[2,3,4,72,384]{4,3,2,0,1:T(8,128)(2,1)} %dynamic-slice_bitcast_fusion), channel_id=1, source_target_pairs={{0,16},{16,0},{1,17},{17,1},{2,18},{18,2},{3,19},{19,3},{4,20},{20... | collective-permute-start | bytes 3981320 | tf_op jit(solution)/shard_map/ppermute | solution.py:53
  183.8 13.1 %all-to-all-start.4 = ((bf16[4,128,576]{1,2,0:T(8,128)(2,1)}), bf16[4,128,576]{1,2,0:T(8,128)(2,1)}, u32[]{:S(2)}, u32[]{:S(2)}) async-start(bf16[4,128,576]{1,2,0:T(8,128)(2,1)} %bitcast.528), calls=%async_computation.4 | async-start | bytes 1179648 | tf_op jit(solution)/shard_map/all_to_all | solution.py:292
  200.5 4.6 %collective-permute-start.13 = (bf16[128,576]{0,1:T(8,128)(2,1)S(1)}, bf16[128,576]{0,1:T(8,128)(2,1)S(1)}, u32[]{:S(2)}, u32[]{:S(2)}) collective-permute-start(bf16[128,576]{0,1:T(8,128)(2,1)S(1)} %get-tuple-element.72), channel_id=1, source_target_pairs={{0,4},{4,0},{8,12},{12,8},{1,5},{5,1},{9,13},{13,9},{2,6},{6,2},{1... | collective-permute-start | bytes 442376 | tf_op jit(solution)/shard_map/ppermute | solution.py:53
  201.8 21.4 %collective-permute-start.14 = (bf16[4,4,72,384]{3,2,1,0:T(8,128)(2,1)S(1)}, bf16[4,4,72,384]{3,2,1,0:T(8,128)(2,1)S(1)}, u32[]{:S(2)}, u32[]{:S(2)}) collective-permute-start(bf16[4,4,72,384]{3,2,1,0:T(8,128)(2,1)S(1)} %dynamic-slice_bitcast_fusion.2), channel_id=1, source_target_pairs={{0,16},{16,0},{1,17},{17,1},{2,18},{18,2},{3,19},{19,3},{4,20},{20... | collective-permute-start | bytes 2654216 | tf_op jit(solution)/shard_map/ppermute | solution.py:53
  202.9 16.5 %collective-permute-start.16 = (bf16[3,4,72,384]{3,2,1,0:T(8,128)(2,1)S(1)}, bf16[3,4,72,384]{3,2,1,0:T(8,128)(2,1)S(1)}, u32[]{:S(2)}, u32[]{:S(2)}) collective-permute-start(bf16[3,4,72,384]{3,2,1,0:T(8,128)(2,1)S(1)} %copy-done.56), channel_id=1, source_target_pairs={{0,8},{4,12},{8,0},{12,4},{1,9},{5,13},{9,1},{13,5},{2,10},{6,14},... | collective-permute-start | bytes 1990664 | tf_op jit(solution)/shard_map/ppermute | solution.py:53
  212.5 59.2 %collective-permute-start.20 = (bf16[2,3,4,72,384]{4,3,1,2,0:T(8,128)(2,1)}, bf16[2,3,4,72,384]{4,3,1,2,0:T(8,128)(2,1)}, u32[]{:S(2)}, u32[]{:S(2)}) collective-permute-start(bf16[2,3,4,72,384]{4,3,1,2,0:T(8,128)(2,1)} %bitcast.476), channel_id=1, source_target_pairs={{0,16},{16,0},{1,17},{17,1},{2,18},{18,2},{3,19},{19,3},{4,20},{20... | collective-permute-start | bytes 3981320 | tf_op jit(solution)/shard_map/ppermute | solution.py:53
  219.6 6.9 %collective-permute-start.19 = (bf16[3,72,384]{2,1,0:T(8,128)(2,1)S(1)}, bf16[3,72,384]{2,1,0:T(8,128)(2,1)S(1)}, u32[]{:S(2)}, u32[]{:S(2)}) collective-permute-start(bf16[3,72,384]{2,1,0:T(8,128)(2,1)S(1)} %get-tuple-element.116), channel_id=1, source_target_pairs={{0,3},{1,2},{2,1},{3,0},{4,7},{5,6},{6,5},{7,4},{8,11},{9,10},{10,... | collective-permute-start | bytes 497672 | tf_op jit(solution)/shard_map/ppermute | solution.py:53
  221.9 14.0 %collective-permute-start.18 = (bf16[3,72,384]{2,1,0:T(8,128)(2,1)S(1)}, bf16[3,72,384]{2,1,0:T(8,128)(2,1)S(1)}, u32[]{:S(2)}, u32[]{:S(2)}) collective-permute-start(bf16[3,72,384]{2,1,0:T(8,128)(2,1)S(1)} %get-tuple-element.117), channel_id=1, source_target_pairs={{0,2},{1,3},{2,0},{3,1},{4,6},{5,7},{6,4},{7,5},{8,10},{9,11},{10,... | collective-permute-start | bytes 497672 | tf_op jit(solution)/shard_map/ppermute | solution.py:53
  221.9 14.0 %collective-permute-start.17 = (bf16[3,72,384]{2,1,0:T(8,128)(2,1)S(1)}, bf16[3,72,384]{2,1,0:T(8,128)(2,1)S(1)}, u32[]{:S(2)}, u32[]{:S(2)}) collective-permute-start(bf16[3,72,384]{2,1,0:T(8,128)(2,1)S(1)} %get-tuple-element.115), channel_id=1, source_target_pairs={{0,1},{1,0},{2,3},{3,2},{4,5},{5,4},{6,7},{7,6},{8,9},{9,8},{10,11... | collective-permute-start | bytes 497672 | tf_op jit(solution)/shard_map/ppermute | solution.py:53
  224.4 18.4 %copy-start.7 = (f32[128,576]{0,1:T(8,128)S(1)}, f32[128,576]{0,1:T(8,128)}, u32[]{:S(2)}) copy-start(f32[128,576]{0,1:T(8,128)} %copy-done.6) | copy-start | bytes 884740
  224.4 18.4 %copy-start.29 = (f32[256,576]{0,1:T(8,128)S(1)}, f32[256,576]{0,1:T(8,128)}, u32[]{:S(2)}) copy-start(f32[256,576]{0,1:T(8,128)} %copy-done.28) | copy-start | bytes 1769476
  224.4 18.4 %copy-start.87 = (f32[576]{0:T(1024)S(1)}, f32[576]{0:T(1024)}, u32[]{:S(2)}) copy-start(f32[576]{0:T(1024)} %copy-done.86) | copy-start | bytes 6916
  224.4 18.4 %copy-start.101 = (f32[128]{0:T(128)S(1)}, f32[128]{0:T(128)}, u32[]{:S(2)}) copy-start(f32[128]{0:T(128)} %copy-done.100) | copy-start | bytes 1540
  224.4 18.7 %copy-start.52 = (f32[128,576]{0,1:T(8,128)S(1)}, f32[128,576]{0,1:T(8,128)}, u32[]{:S(2)}) copy-start(f32[128,576]{0,1:T(8,128)} %get-tuple-element.73) | copy-start | bytes 884740
  224.4 18.4 %collective-permute-start.15 = (bf16[128,576]{0,1:T(8,128)(2,1)}, bf16[128,576]{0,1:T(8,128)(2,1)S(1)}, u32[]{:S(2)}, u32[]{:S(2)}) collective-permute-start(bf16[128,576]{0,1:T(8,128)(2,1)} %slice.441), channel_id=1, source_target_pairs={{0,4},{4,0},{8,12},{12,8},{1,5},{5,1},{9,13},{13,9},{2,6},{6,2},{1... | collective-permute-start | bytes 442376 | tf_op jit(solution)/shard_map/ppermute | solution.py:53
  236.7 24.3 %collective-permute-start.33 = (f32[3,72,384]{2,1,0:T(8,128)}, f32[3,72,384]{2,1,0:T(8,128)}, u32[]{:S(2)}, u32[]{:S(2)}) collective-permute-start(f32[3,72,384]{2,1,0:T(8,128)} %fusion.68), channel_id=1, source_target_pairs={{0,16},{16,0},{1,17},{17,1},{2,18},{18,2},{3,19},{19,3},{4,20},{20... | collective-permute-start | bytes 995336 | tf_op jit(solution)/shard_map/ppermute | solution.py:53
  238.4 16.5 %all-to-all-start.5 = ((bf16[4,4,72,384]{3,2,1,0:T(8,128)(2,1)}), bf16[4,4,72,384]{3,2,1,0:T(8,128)(2,1)}, u32[]{:S(2)}, u32[]{:S(2)}) async-start(bf16[4,4,72,384]{3,2,1,0:T(8,128)(2,1)} %fusion.13), calls=%async_computation.5 | async-start | bytes 1769472 | tf_op jit(solution)/shard_map/all_to_all | solution.py:311
  256.9 9.6 %all-to-all-start.8 = ((bf16[4,72,384]{2,1,0:T(8,128)(2,1)}), bf16[4,72,384]{2,1,0:T(8,128)(2,1)}, u32[]{:S(2)}, u32[]{:S(2)}) async-start(bf16[4,72,384]{2,1,0:T(8,128)(2,1)} %reduce_sum.207), calls=%async_computation.8 | async-start | bytes 442368 | tf_op jit(solution)/shard_map/all_to_all | solution.py:314
  268.1 22.3 %collective-permute-start.27 = (f32[72,384]{1,0:T(8,128)}, f32[72,384]{1,0:T(8,128)}, u32[]{:S(2)}, u32[]{:S(2)}) collective-permute-start(f32[72,384]{1,0:T(8,128)} %convert_reduce_fusion.2), channel_id=1, source_target_pairs={{0,16},{16,0},{1,17},{17,1},{2,18},{18,2},{3,19},{19,3},{4,20},{20... | collective-permute-start | bytes 331784 | tf_op jit(solution)/shard_map/ppermute | solution.py:53
  281.7 28.5 %collective-permute-start.23 = (bf16[128,576]{0,1:T(8,128)(2,1)}, bf16[128,576]{0,1:T(8,128)(2,1)}, u32[]{:S(2)}, u32[]{:S(2)}) collective-permute-start(bf16[128,576]{0,1:T(8,128)(2,1)} %bitcast.478), channel_id=1, source_target_pairs={{0,12},{4,8},{8,4},{12,0},{1,13},{5,9},{9,5},{13,1},{2,14},{6,10},... | collective-permute-start | bytes 442376 | tf_op jit(solution)/shard_map/ppermute | solution.py:53
  283.5 33.8 %collective-permute-start.22 = (bf16[128,576]{0,1:T(8,128)(2,1)}, bf16[128,576]{0,1:T(8,128)(2,1)}, u32[]{:S(2)}, u32[]{:S(2)}) collective-permute-start(bf16[128,576]{0,1:T(8,128)(2,1)} %bitcast.479), channel_id=1, source_target_pairs={{0,8},{4,12},{8,0},{12,4},{1,9},{5,13},{9,1},{13,5},{2,10},{6,14},... | collective-permute-start | bytes 442376 | tf_op jit(solution)/shard_map/ppermute | solution.py:53
  284.7 5.3 %collective-permute-start.25 = (f32[2,2,576]{2,1,0:T(2,128)S(1)}, f32[2,2,576]{2,1,0:T(2,128)S(1)}, u32[]{:S(2)}, u32[]{:S(2)}) collective-permute-start(f32[2,2,576]{2,1,0:T(2,128)S(1)} %pad_maximum_fusion.32), channel_id=1, source_target_pairs={{0,16},{16,0},{1,17},{17,1},{2,18},{18,2},{3,19},{19,3},{4,20},{20... | collective-permute-start | bytes 27656 | tf_op jit(solution)/shard_map/ppermute | solution.py:53
  288.0 18.1 %copy-start.20 = (bf16[2,3,4,72,384]{4,3,1,2,0:T(8,128)(2,1)S(1)}, bf16[2,3,4,72,384]{4,3,1,2,0:T(8,128)(2,1)}, u32[]{:S(2)}) copy-start(bf16[2,3,4,72,384]{4,3,1,2,0:T(8,128)(2,1)} %copy-done.19) | copy-start | bytes 3981316
  288.0 18.1 %collective-permute-start.28 = (bf16[3,4,72,384]{3,2,0,1:T(8,128)(2,1)}, bf16[3,4,72,384]{3,2,0,1:T(8,128)(2,1)}, u32[]{:S(2)}, u32[]{:S(2)}) collective-permute-start(bf16[3,4,72,384]{3,2,0,1:T(8,128)(2,1)} %slice_bitcast_fusion), channel_id=1, source_target_pairs={{0,8},{4,12},{8,0},{12,4},{1,9},{5,13},{9,1},{13,5},{2,10},{6,14},... | collective-permute-start | bytes 1990664 | tf_op jit(solution)/shard_map/ppermute | solution.py:53
  290.0 18.6 %collective-permute-start.24 = (bf16[4,4,72,384]{3,2,1,0:T(8,128)(2,1)}, bf16[4,4,72,384]{3,2,1,0:T(8,128)(2,1)}, u32[]{:S(2)}, u32[]{:S(2)}) collective-permute-start(bf16[4,4,72,384]{3,2,1,0:T(8,128)(2,1)} %dynamic-slice_bitcast_fusion.1), channel_id=1, source_target_pairs={{0,16},{16,0},{1,17},{17,1},{2,18},{18,2},{3,19},{19,3},{4,20},{20... | collective-permute-start | bytes 2654216 | tf_op jit(solution)/shard_map/ppermute | solution.py:53
  290.4 26.9 %collective-permute-start.21 = (bf16[128,576]{0,1:T(8,128)(2,1)}, bf16[128,576]{0,1:T(8,128)(2,1)S(1)}, u32[]{:S(2)}, u32[]{:S(2)}) collective-permute-start(bf16[128,576]{0,1:T(8,128)(2,1)} %bitcast.568), channel_id=1, source_target_pairs={{0,4},{4,0},{8,12},{12,8},{1,5},{5,1},{9,13},{13,9},{2,6},{6,2},{1... | collective-permute-start | bytes 442376 | tf_op jit(solution)/shard_map/ppermute | solution.py:53
  307.4 11.1 %collective-permute-start.31 = (bf16[3,72,384]{2,1,0:T(8,128)(2,1)S(1)}, bf16[3,72,384]{2,1,0:T(8,128)(2,1)S(1)}, u32[]{:S(2)}, u32[]{:S(2)}) collective-permute-start(bf16[3,72,384]{2,1,0:T(8,128)(2,1)S(1)} %get-tuple-element.113), channel_id=1, source_target_pairs={{0,3},{1,2},{2,1},{3,0},{4,7},{5,6},{6,5},{7,4},{8,11},{9,10},{10,... | collective-permute-start | bytes 497672 | tf_op jit(solution)/shard_map/ppermute | solution.py:53
  308.6 14.7 %collective-permute-start.30 = (bf16[3,72,384]{2,1,0:T(8,128)(2,1)S(1)}, bf16[3,72,384]{2,1,0:T(8,128)(2,1)S(1)}, u32[]{:S(2)}, u32[]{:S(2)}) collective-permute-start(bf16[3,72,384]{2,1,0:T(8,128)(2,1)S(1)} %get-tuple-element.114), channel_id=1, source_target_pairs={{0,2},{1,3},{2,0},{3,1},{4,6},{5,7},{6,4},{7,5},{8,10},{9,11},{10,... | collective-permute-start | bytes 497672 | tf_op jit(solution)/shard_map/ppermute | solution.py:53
  310.2 13.1 %collective-permute-start.29 = (bf16[3,72,384]{2,1,0:T(8,128)(2,1)S(1)}, bf16[3,72,384]{2,1,0:T(8,128)(2,1)S(1)}, u32[]{:S(2)}, u32[]{:S(2)}) collective-permute-start(bf16[3,72,384]{2,1,0:T(8,128)(2,1)S(1)} %get-tuple-element.112), channel_id=1, source_target_pairs={{0,1},{1,0},{2,3},{3,2},{4,5},{5,4},{6,7},{7,6},{8,9},{9,8},{10,11... | collective-permute-start | bytes 497672 | tf_op jit(solution)/shard_map/ppermute | solution.py:53
  313.7 16.0 %all-to-all-start.6 = ((bf16[4,4,80,384]{3,2,1,0:T(8,128)(2,1)}), bf16[4,4,80,384]{3,2,1,0:T(8,128)(2,1)S(1)}, u32[]{:S(2)}, u32[]{:S(2)}) async-start(bf16[4,4,80,384]{3,2,1,0:T(8,128)(2,1)} %pad_maximum_fusion.8), calls=%async_computation.6 | async-start | bytes 1966080 | tf_op jit(solution)/shard_map/all_to_all | solution.py:311
  324.3 9.7 %collective-permute-start.32 = (f32[3,72,384]{2,1,0:T(8,128)S(1)}, f32[3,72,384]{2,1,0:T(8,128)S(1)}, u32[]{:S(2)}, u32[]{:S(2)}) collective-permute-start(f32[3,72,384]{2,1,0:T(8,128)S(1)} %fusion.66), channel_id=1, source_target_pairs={{0,16},{16,0},{1,17},{17,1},{2,18},{18,2},{3,19},{19,3},{4,20},{20... | collective-permute-start | bytes 995336 | tf_op jit(solution)/shard_map/ppermute | solution.py:53
  330.5 9.0 %all-to-all-start.7 = ((bf16[4,80,384]{2,1,0:T(8,128)(2,1)}), bf16[4,80,384]{2,1,0:T(8,128)(2,1)S(1)}, u32[]{:S(2)}, u32[]{:S(2)}) async-start(bf16[4,80,384]{2,1,0:T(8,128)(2,1)} %reduce_sum.213), calls=%async_computation.7 | async-start | bytes 491520 | tf_op jit(solution)/shard_map/all_to_all | solution.py:314
  339.5 5.7 %collective-permute-start.26 = (f32[72,384]{1,0:T(8,128)S(1)}, f32[72,384]{1,0:T(8,128)S(1)}, u32[]{:S(2)}, u32[]{:S(2)}) collective-permute-start(f32[72,384]{1,0:T(8,128)S(1)} %slice.305), channel_id=1, source_target_pairs={{0,16},{16,0},{1,17},{17,1},{2,18},{18,2},{3,19},{19,3},{4,20},{20... | collective-permute-start | bytes 331784 | tf_op jit(solution)/shard_map/ppermute | solution.py:53
  (86 other events, 306.2 us)
Sparse Core Ops, SparseCore 0:
  18.5 34.0 all-gather.2
where the time goes:
time: 359 us; the launch traced here: 354 us
  starting transfers between devices  87.5 us (24%)
  waiting for transfers between devices  79.5 us (22%)
  matrix products  55.7 us (16%)
  other arithmetic  49.2 us (14%)
  local copies, waits for them, and re-layouts  41.4 us (12%)
  blocking collectives  24.1 us (7%)
  between operations  16.8 us (5%)
    ppermute x34, waiting for transfers between devices, swap(): lax.ppermute(values, axis, [(i, i ^ bit) for i in range(lax.axis_size(axi...  54 us
    ppermute x34, starting transfers between devices, swap(): lax.ppermute(values, axis, [(i, i ^ bit) for i in range(lax.axis_size(axi...  51.2 us
    dot_general x40, matrix products, mm(): return jnp.einsum(spec, left, right, preferred_element_type=f32)  48.6 us
    all_to_all x4, starting transfers between devices, spread(): return lax.all_to_all(copies, axis, 0, 0, tiled=True)  16.7 us
    all_gather x1, blocking collectives, on_device(): resid_all = lax.all_gather(hidden_in, 'row', axis=0, tiled=True).astype(f32)  15.6 us
    unnamed x217, local copies, waits for them, and re-layouts  13.3 us
    all_to_all x2, waiting for transfers between devices, on_device(): attn_grad = lax.all_to_all(attn_grad, 'col', 0, 0, tiled=True)  8.83 us
    all_gather x1, blocking collectives, on_device(): normed_all = lax.all_gather(normed1, 'row', axis=0, tiled=True)  8.45 us
  transfers between devices with their start and end apart: 44, of which 17 were waited for; matrix products, arithmetic and copies ran while one was open for 34% of the time, Pallas kernels for 0%

commit v1 on v0

--- a/solution.py
+++ b/solution.py
@@ -22,9 +22,9 @@
     return jnp.einsum(spec, left, right, preferred_element_type=f32)
 
 
-def rope_tables(first_place, amount):
+def rope_tables(token_places):
     half_dim = HEAD_DIM // 2
-    places = (first_place + jnp.arange(amount)).astype(f32)
+    places = token_places.astype(f32)
     frequency = rope_base ** (-(2.0 * jnp.arange(half_dim).astype(f32)) / HEAD_DIM)
     angles = places[:, None] * frequency[None, :]
     return (jnp.cos(angles)[:, None, :], jnp.sin(angles)[:, None, :])
@@ -53,9 +53,48 @@
     return lax.ppermute(values, axis, [(i, i ^ bit) for i in range(lax.axis_size(axis))])
 
 
+def neighbours(values, axis):
+    return [values] + [swap(values, axis, bits) for bits in range(1, lax.axis_size(axis))]
+
+
+def in_order(blocks, axis):
+    place = lax.axis_index(axis)
+    held = jnp.stack(blocks, 0)
+    return jnp.stack(
+        [
+            lax.dynamic_index_in_dim(held, place ^ index, 0, keepdims=False)
+            for index in range(len(blocks))
+        ],
+        0,
+    )
+
+
 def spread(values, axis):
-    copies = jnp.broadcast_to(values[None], (lax.axis_size(axis),) + values.shape)
+    size = lax.axis_size(axis)
+    copies = jnp.broadcast_to(values[None], (size,) + values.shape)
     return lax.all_to_all(copies, axis, 0, 0, tiled=True)
+
+
+def feed_whole(block, core, size_row, size_col):
+    halves = block.reshape(3, 2, block.shape[1] // 2, block.shape[2])
+    mine = lax.dynamic_index_in_dim(halves, core, 1, keepdims=False)
+    size = lax.axis_size("dp")
+    groups = [
+        [
+            ((2 * pair + data) * size_row + high * 2 + low) * size_col + column
+            for high in range(2)
+            for column in range(size_col)
+            for data in range(2)
+        ]
+        for pair in range(size // 2)
+        for low in range(2)
+    ]
+    whole = lax.all_gather(mine, ("dp", "row", "col"), axis=0, axis_index_groups=groups)
+    return whole.reshape((2, size_col, 2) + mine.shape)
+
+
+def exchange_sum(values, axes):
+    return jnp.sum(lax.all_to_all(values, axes, 0, 0, tiled=True).astype(f32), 0)
 
 
 def scatter_sum(values, axis):
@@ -68,13 +107,22 @@
 
 
 def after(values, *earlier):
-    return lax.optimization_barrier((values,) + earlier)[0]
+    zero = 0.0
+    for array in earlier:
+        first = array[(0,) * array.ndim].astype(f32)
+        zero = zero + jnp.minimum(jnp.abs(first), 0.0)
+    return values + zero.astype(values.dtype)
 
 
 def merge_halves(own, other, core):
     low = jnp.where(core == 0, own, other)
     high = jnp.where(core == 0, other, own)
     return jnp.stack([low, high], -3)
+
+
+def joined(part, core):
+    whole = merge_halves(part, swap(part, "dp", 1), core)
+    return whole.reshape(whole.shape[0], -1, whole.shape[-1])
 
 
 def sum_pairs(values):
@@ -98,7 +146,6 @@
     size_row = lax.axis_size("row")
     size_col = lax.axis_size("col")
     core = lax.axis_index("dp") % 2
-    first_place = lax.axis_index("row") * rows
     pack = rows * size_row
     length = lengths[0]
     layers, deep, wide_qkv = w_qkv.shape
@@ -111,49 +158,45 @@
     attn_blocks = jnp.concatenate([w_qkv, jnp.swapaxes(w_out, 1, 2)], -1)
     attn_half = lax.dynamic_slice_in_dim(attn_blocks, core * half, half, 1)
     feed_blocks = jnp.stack([w_gate, w_up, jnp.swapaxes(w_down, 1, 2)], 1)
-    feed_half = lax.dynamic_slice_in_dim(feed_blocks, core * half, half, 2)
-    full_attn, full_gate, full_up, full_down = [], [], [], []
-    part = None
+    hidden_blocks = neighbours(hidden_in, "row")
+    attn_cols = in_order(neighbours(attn_half, "col"), "col")
+    full_attn, feed_parts = [], []
     for layer in range(layers):
-        mine = attn_half[layer] if part is None else after(attn_half[layer], part)
-        part = spread(spread(mine, "col"), "row")
-        whole = merge_halves(part, swap(part, "dp", 1), core)
-        full_attn.append(whole.reshape(size_row, D, both))
-    feed_parts = lax.all_gather(feed_half, "col", axis=2)
-    for layer in range(layers):
-        part = feed_parts[layer]
-        part = jnp.stack([part, swap(part, "row", 2)], 1)
-        whole = merge_halves(part, swap(part, "dp", 1), core).reshape(3, 2, D, wide)
-        full_gate.append(whole[0])
-        full_up.append(whole[1])
-        full_down.append(whole[2])
-
-    cosine, sine_vals = rope_tables(0, pack)
-    own_cosine, own_sine = rope_tables(first_place, rows)
-    key_places = jnp.arange(pack)
-    query_places = first_place + jnp.arange(rows)
+        if layer == 0:
+            part = spread(after(attn_cols[:, layer], *hidden_blocks[1:]), "row")
+            full_attn.append(joined(part, core))
+        else:
+            full_attn.append(spread(after(attn_cols[:, layer], full_attn[0]), "row"))
+        feed_parts.append(feed_whole(feed_blocks[layer], core, size_row, size_col))
+    full_gate, full_up, full_down = [], [], []
+
+    place = lax.axis_index("row")
+    key_places = jnp.concatenate(
+        [(place ^ bits) * rows + jnp.arange(rows) for bits in range(size_row)], 0
+    )
+    cosine, sine_vals = rope_tables(key_places)
+    own_cosine, own_sine = cosine[:rows], sine_vals[:rows]
+    query_places = key_places[:rows]
     visible = (key_places[None, :] <= query_places[:, None]) & (key_places[None, :] < length)
 
-    def own_rows(values):
-        return lax.dynamic_slice_in_dim(values, first_place, rows, 0)
-
     resid = hidden_in.astype(f32)
-    both_cotangent = jnp.concatenate([cotangent, swap(cotangent, "row", 1)], 0)
+    late_cotangent = after(cotangent, full_attn[0])
+    both_cotangent = jnp.concatenate([cotangent, swap(late_cotangent, "row", 1)], 0)
     stored = []
     for layer in range(layers):
         if layer == 0:
-            resid_all = lax.all_gather(hidden_in, "row", axis=0, tiled=True).astype(f32)
+            resid_all = jnp.concatenate(hidden_blocks, 0).astype(f32)
             inverse_all = lax.rsqrt(jnp.mean(resid_all * resid_all, -1, keepdims=True) + eps_norm)
             scaled_all = resid_all * inverse_all
             normed_all = (scaled_all * gains[layer, 0]).astype(bf16)
-            inverse1 = own_rows(inverse_all)
+            inverse1 = inverse_all[:rows]
         else:
             inverse1 = lax.rsqrt(jnp.mean(resid * resid, -1, keepdims=True) + eps_norm)
             normed1 = (resid * inverse1 * gains[layer, 0]).astype(bf16)
-            normed_all = lax.all_gather(normed1, "row", axis=0, tiled=True)
+            normed_all = jnp.concatenate(neighbours(normed1, "row"), 0)
         mixed = mm("td,rdk->trk", normed_all, full_attn[layer])[:, :, :wide_qkv]
         mixed = mixed.astype(bf16).reshape(pack, QKV)
-        query = own_rows(mixed[:, :D]).astype(f32).reshape(rows, HEADS, HEAD_DIM)
+        query = mixed[:rows, :D].astype(f32).reshape(rows, HEADS, HEAD_DIM)
         query_rot = rotate(query, own_cosine, own_sine).astype(bf16)
         query_rot = query_rot.reshape(rows, KV_HEADS, GROUP, HEAD_DIM)
         keys = mixed[:, D : D + KV].astype(f32).reshape(pack, KV_HEADS, HEAD_DIM)
@@ -172,6 +215,12 @@
         inverse2 = lax.rsqrt(jnp.mean(resid_mid * resid_mid, -1, keepdims=True) + eps_norm)
         normed2 = (resid_mid * inverse2 * gains[layer, 1]).astype(bf16)
         both_normed2 = jnp.concatenate([normed2, swap(normed2, "row", 1)], 0)
+        feed = after(feed_parts[layer], normed2)
+        full_gate.append(feed[:, :, :, 0].reshape(2, D, wide))
+        full_up.append(feed[:, :, :, 1].reshape(2, D, wide))
+        full_down.append(feed[:, :, :, 2].reshape(2, D, wide))
+        if layer + 1 < layers:
+            full_attn[layer + 1] = joined(after(full_attn[layer + 1], normed2), core)
         gate_act = mm("td,bdf->tbf", both_normed2, full_gate[layer])
         up_act = mm("td,bdf->tbf", both_normed2, full_up[layer])
         hidden = (gate_act * jax.nn.sigmoid(gate_act) * up_act).astype(bf16)
@@ -202,7 +251,6 @@
     attn_grads = [None] * layers
     feed_grads = [None] * layers
     gain_grads = [None] * layers
-    waiting = {}
     for layer in reversed(range(layers)):
         (
             resid_in,
@@ -225,17 +273,13 @@
         else:
             grad_low = grad_resid.astype(bf16)
             both_grad = jnp.concatenate([grad_low, swap(grad_low, "row", 1)], 0)
-            both_grad = after(both_grad, waiting["feed_two"])
         grad_hid = mm("td,bdf->tbf", both_grad, full_down[layer])
         sigma = jax.nn.sigmoid(gate_act)
         grad_gate_act = (grad_hid * up_act * sigma * (1.0 + gate_act * (1.0 - sigma))).astype(bf16)
         grad_up_act = (grad_hid * gate_act * sigma).astype(bf16)
         norm2_part = mm("tbf,bdf->td", grad_gate_act, full_gate[layer])
         norm2_part = norm2_part + mm("tbf,bdf->td", grad_up_act, full_up[layer])
-        moved = norm2_part[rows:].astype(bf16)
-        if waiting:
-            moved = after(moved, waiting["attn_half"])
-        moved = swap(moved, "row", 1).astype(f32)
+        moved = swap(norm2_part[rows:].astype(bf16), "row", 1).astype(f32)
         grad_norm2 = norm2_part[:rows] + moved
         feed_grad = jnp.stack(
             [
@@ -246,17 +290,16 @@
             1,
         )
         feed_half_sum = halve(feed_grad.reshape(2, 3, size_col, 2, half, wide), core)
-        feed_two = feed_half_sum[0].astype(f32) + swap(feed_half_sum[1], "row", 2).astype(f32)
-        feed_two = jnp.swapaxes(feed_two.astype(bf16), 0, 1)
-        feed_grad = scatter_sum(feed_two, "col")
-        other = swap(feed_grad, "dp", 1)
-        feed_grads[layer] = merge_halves(feed_grad, other, core).reshape(3, deep, wide)
+        keep = lax.dynamic_index_in_dim(feed_half_sum, place // 2, 0, keepdims=False)
+        send = lax.dynamic_index_in_dim(feed_half_sum, 1 - place // 2, 0, keepdims=False)
+        feed_two = keep.astype(f32) + swap(send, "row", 2).astype(f32)
+        feed_two = jnp.swapaxes(feed_two, 0, 1).astype(bf16).reshape(-1, wide)
+        feed_grad = lax.psum_scatter(feed_two, "col", scatter_dimension=0, tiled=True)
+        feed_grads[layer] = feed_grad.reshape(3, half, wide)
 
         gain_grad2 = jnp.sum(grad_norm2 * (resid_mid * inverse2), 0)
         grad_resid = grad_resid + norm_back(resid_mid, inverse2, gains[layer, 1], grad_norm2)
-        grad_low = grad_resid.astype(bf16)
-        if waiting:
-            grad_low = after(grad_low, waiting["feed_grad"])
+        grad_low = after(grad_resid, feed_half_sum).astype(bf16)
         grad_att = mm("td,rdk->trk", grad_low, full_attn[layer])[:, :, wide_qkv:].astype(bf16)
         grad_att = grad_att.reshape(rows, KV_HEADS, GROUP, HEAD_DIM)
         grad_out = mm("td,trk->rdk", grad_low, attended_blocks)
@@ -269,9 +312,7 @@
         grad_query = rotate(grad_query.reshape(rows, HEADS, HEAD_DIM), own_cosine, -own_sine)
         grad_keys = rotate(grad_keys, cosine, -sine_vals)
         grad_query = grad_query.reshape(rows, D).astype(bf16)
-        grad_query = lax.dynamic_update_slice_in_dim(
-            jnp.zeros((pack, D), bf16), grad_query, first_place, 0
-        )
+        grad_query = jnp.pad(grad_query, ((0, pack - rows), (0, 0)))
         grad_mixed = jnp.concatenate(
             [
                 grad_query,
@@ -281,25 +322,25 @@
             -1,
         ).reshape(pack, size_row, wide_qkv)
         grad_mixed = jnp.pad(grad_mixed, ((0, 0), (0, 0), (0, wide_out)))
-        grad_mixed = after(grad_mixed, feed_half_sum)
-        if waiting:
-            grad_mixed = after(grad_mixed, waiting["attn_row"])
         norm1_part = mm("trk,rdk->td", grad_mixed, full_attn[layer])
-        norm1_blocks = norm1_part.astype(bf16).reshape(size_row, rows, D)
-        if layer == 0:
-            grad_norm1 = scatter_sum(norm1_blocks, "row")
-        else:
-            grad_norm1 = lax.all_to_all(norm1_blocks, "row", 0, 0, tiled=True)
-            grad_norm1 = jnp.sum(grad_norm1.astype(f32), 0)
+        grad_norm1 = norm1_part[:rows]
+        norm1_low = norm1_part.astype(bf16)
+        for bits in range(1, size_row):
+            moved = swap(norm1_low[bits * rows : (bits + 1) * rows], "row", bits)
+            grad_norm1 = grad_norm1 + moved.astype(f32)
         if layer == 0:
             gain_grad1 = jnp.sum(norm1_part * scaled_all, 0)
         else:
             gain_grad1 = jnp.sum(grad_norm1 * (resid_in * inverse1), 0)
         grad_resid = grad_resid + norm_back(resid_in, inverse1, gains[layer, 0], grad_norm1)
         gain_grads[layer] = jnp.stack([gain_grad1, gain_grad2], 0)
-        attn_grad = (mm("td,trk->rdk", normed_all, grad_mixed) + grad_out).astype(bf16)
+        attn_grad = mm("td,trk->rdk", normed_all, grad_mixed) + grad_out
+        attn_grad = after(attn_grad, feed_two).astype(bf16)
         attn_grad = halve(attn_grad.reshape(size_row, size_col, 2, half, both), core)
-        if layer == 0:
+        if layer > 0:
+            attn_grad = attn_grad.reshape(size_row * size_col, half, both)
+            attn_grads[layer] = exchange_sum(attn_grad, ("row", "col")).astype(bf16)
+        else:
             gain_part = jnp.stack(gain_grads, 0)
             gain_part = sum_pairs((gain_part + swap(gain_part, "dp", 1)).astype(bf16))
             gain_rows = gain_part.reshape(-1, both)
@@ -307,29 +348,27 @@
             gain_rows = jnp.pad(gain_rows, ((0, -extra % 8), (0, 0)))
             gain_rows = jnp.broadcast_to(gain_rows, (size_row, size_col) + gain_rows.shape)
             attn_grad = jnp.concatenate([attn_grad, gain_rows], 2)
-        waiting = {"feed_two": feed_two, "feed_grad": feed_grad, "attn_half": attn_grad}
-        attn_grad = lax.all_to_all(attn_grad, "row", 0, 0, tiled=True)
-        attn_grad = jnp.sum(attn_grad.astype(f32), 0).astype(bf16)
-        waiting["attn_row"] = attn_grad
-        attn_grad = lax.all_to_all(attn_grad, "col", 0, 0, tiled=True)
-        attn_grad = jnp.sum(attn_grad.astype(f32), 0)
-        if layer == 0:
+            attn_grad = scatter_sum(attn_grad, "row").astype(bf16)
+            last = attn_grad
+            attn_grad = scatter_sum(attn_grad, "col")
             gain_total = attn_grad[half : half + extra].reshape(layers, 2, D)
-            attn_grad = attn_grad[:half]
-        other = swap(attn_grad, "dp", 1)
-        attn_grads[layer] = merge_halves(attn_grad, other, core).reshape(deep, -1)
-
-    attn_grads = jnp.stack(attn_grads, 0)
-    feed_grads = jnp.stack(feed_grads, 0)
+            attn_grads[layer] = attn_grad[:half].astype(bf16)
+
+    own = [
+        jnp.concatenate([attn_grads[layer][None], feed_grads[layer]], 0) for layer in range(layers)
+    ]
+    own = after(jnp.stack(own, 0), last)
+    grads = merge_halves(own, swap(own, "dp", 1), core).astype(f32)
+    grads = grads.reshape(layers, 4, deep, both)
     return (
         resid.astype(bf16),
         grad_resid,
         gain_total,
-        attn_grads[:, :, :wide_qkv],
-        jnp.swapaxes(attn_grads[:, :, wide_qkv:], 1, 2),
-        feed_grads[:, 0],
-        feed_grads[:, 1],
-        jnp.swapaxes(feed_grads[:, 2], 1, 2),
+        grads[:, 0, :, :wide_qkv],
+        jnp.swapaxes(grads[:, 0, :, wide_qkv:], 1, 2),
+        grads[:, 1],
+        grads[:, 2],
+        jnp.swapaxes(grads[:, 3], 1, 2),
     )
 
 

time: 359 us -> 320 us (0.89)
  starting transfers between devices: 87.5 us -> 58.3 us
  blocking collectives: 24.1 us -> 0 us
  matrix products: 55.7 us -> 74.6 us
  other arithmetic: 49.2 us -> 41.2 us
  between operations: 16.8 us -> 24.6 us
    all_gather x2 -> x0, blocking collectives: 24.1 us -> none  [the longest x1 15.6 us: on_device(): resid_all = lax.all_gather(hidden_in, 'row', axis=0, tiled=True).astype(f32)]
    dot_general x40, matrix products: 48.6 us -> 68.4 us  [mm(): return jnp.einsum(spec, left, right, preferred_element_type=f32)]
    all_to_all x5 -> x1, waiting for transfers between devices: 17.1 us -> 0.01 us  [exchange_sum(): lax.all_to_all(values, axes, 0, 0, tiled=True).astype(f32)]
    all_to_all x5 -> x1, starting transfers between devices: 19.6 us -> 4.3 us  [exchange_sum(): lax.all_to_all(values, axes, 0, 0, tiled=True).astype(f32)]
    all_to_all x4 -> x2, waiting for transfers between devices: 8.39 us -> 20.1 us  [spread(): return lax.all_to_all(copies, axis, 0, 0, tiled=True)]
    all_to_all x4 -> x2, starting transfers between devices: 16.7 us -> 7 us  [spread(): return lax.all_to_all(copies, axis, 0, 0, tiled=True)]
    ppermute x34 -> x39, waiting for transfers between devices: 54 us -> 61.2 us  [swap(): lax.ppermute(values, axis, [(i, i ^ bit) for i in range(lax.axis_size(axi...]
    add x1 -> x9, other arithmetic: 0.01 us -> 5.81 us  [the longest x7 5.79 us: after(): return values + zero.astype(values.dtype)]
  transfers between devices with their start and end apart: 44 -> 46, of which waited for: 17 -> 20; matrix products, arithmetic and copies ran while one was open for 34% -> 36% of each run, Pallas kernels for 0% -> 0%
where the time goes in v1:
time: 320 us; the launch traced here: 318 us
  waiting for transfers between devices  81.4 us (25%)
  matrix products  74.6 us (23%)
  starting transfers between devices  58.3 us (18%)
  other arithmetic  41.2 us (13%)
  local copies, waits for them, and re-layouts  38 us (12%)
  between operations  24.6 us (8%)
    dot_general x40, matrix products, mm(): return jnp.einsum(spec, left, right, preferred_element_type=f32)  68.4 us
    ppermute x39, waiting for transfers between devices, swap(): lax.ppermute(values, axis, [(i, i ^ bit) for i in range(lax.axis_size(axi...  61.2 us
    ppermute x39, starting transfers between devices, swap(): lax.ppermute(values, axis, [(i, i ^ bit) for i in range(lax.axis_size(axi...  46.6 us
    all_to_all x2, waiting for transfers between devices, spread(): return lax.all_to_all(copies, axis, 0, 0, tiled=True)  20.1 us
    unnamed x231, local copies, waits for them, and re-layouts  8.3 us
    slice x11, local copies, waits for them, and re-layouts, after(): first = array[(0,) * array.ndim].astype(f32)  7.26 us
    all_to_all x2, starting transfers between devices, spread(): return lax.all_to_all(copies, axis, 0, 0, tiled=True)  7 us
  transfers between devices with their start and end apart: 46, of which 20 were waited for; matrix products, arithmetic and copies ran while one was open for 36% of the time, Pallas kernels for 0%

profile of v1, /device:TPU:1, one launch (start us, length us, event | category | flops | bytes accessed | tf_op | source)
XLA Modules:
  0.0 318.2 jit_solution(13924504522027406036)
XLA Ops:
  9.7 4.2 %collective-permute-start.5 = (bf16[2,72,384]{2,1,0:T(8,128)(2,1)S(1)}, bf16[2,72,384]{2,1,0:T(8,128)(2,1)S(1)}, u32[]{:S(2)}, u32[]{:S(2)}) collective-permute-start(bf16[2,72,384]{2,1,0:T(8,128)(2,1)S(1)} %fusion.107), channel_id=1, source_target_pairs={{0,3},{1,2},{2,1},{3,0},{4,7},{5,6},{6,5},{7,4},{8,11},{9,10},{10,... | collective-permute-start | bytes 331784 | tf_op jit(solution)/shard_map/ppermute | solution.py:53
  18.7 4.1 %collective-permute-done.4 = bf16[2,72,384]{2,1,0:T(8,128)(2,1)S(1)} collective-permute-done((bf16[2,72,384]{2,1,0:T(8,128)(2,1)S(1)}, bf16[2,72,384]{2,1,0:T(8,128)(2,1)S(1)}, u32[]{:S(2)}, u32[]{:S(2)}) %collective-permute-start.4) | collective-permute-done | bytes 110624 | tf_op jit(solution)/shard_map/ppermute | solution.py:53
  27.8 3.5 %all-to-all-start = ((bf16[4,4,72,384]{3,2,1,0:T(8,128)(2,1)}), bf16[4,4,72,384]{3,2,1,0:T(8,128)(2,1)S(1)}, u32[]{:S(2)}, u32[]{:S(2)}) async-start(bf16[4,4,72,384]{3,2,1,0:T(8,128)(2,1)} %broadcast_in_dim.20), calls=%async_computation | async-start | bytes 1769472 | tf_op jit(solution)/shard_map/all_to_all | solution.py:75
  32.3 10.6 %all-to-all-done = bf16[4,4,72,384]{3,2,1,0:T(8,128)(2,1)S(1)} async-done(((bf16[4,4,72,384]{3,2,1,0:T(8,128)(2,1)}), bf16[4,4,72,384]{3,2,1,0:T(8,128)(2,1)S(1)}, u32[]{:S(2)}, u32[]{:S(2)}) %all-to-all-start) | async-done | bytes 884768 | tf_op jit(solution)/shard_map/all_to_all | solution.py:75
  42.9 3.5 %collective-permute-start.6 = (bf16[4,4,72,384]{3,2,1,0:T(8,128)(2,1)S(1)}, bf16[4,4,72,384]{3,2,1,0:T(8,128)(2,1)S(1)}, u32[]{:S(2)}, u32[]{:S(2)}) collective-permute-start(bf16[4,4,72,384]{3,2,1,0:T(8,128)(2,1)S(1)} %all-to-all-done), channel_id=1, source_target_pairs={{0,16},{16,0},{1,17},{17,1},{2,18},{18,2},{3,19},{19,3},{4,20},{20... | collective-permute-start | bytes 2654216 | tf_op jit(solution)/shard_map/ppermute | solution.py:53
  48.9 1.5 fusion.72
  51.4 2.4 fusion.161
  57.6 3.5 %all-to-all-start.1 = ((bf16[4,4,72,384]{3,2,1,0:T(8,128)(2,1)}), bf16[4,4,72,384]{3,2,1,0:T(8,128)(2,1)S(1)}, u32[]{:S(2)}, u32[]{:S(2)}) async-start(bf16[4,4,72,384]{3,2,1,0:T(8,128)(2,1)} %broadcast_in_dim.23), calls=%async_computation.1 | async-start | bytes 1769472 | tf_op jit(solution)/shard_map/all_to_all | solution.py:75
  62.1 1.4 collective-permute-start.7
  64.9 9.5 %all-to-all-done.1 = bf16[4,4,72,384]{3,2,1,0:T(8,128)(2,1)S(1)} async-done(((bf16[4,4,72,384]{3,2,1,0:T(8,128)(2,1)}), bf16[4,4,72,384]{3,2,1,0:T(8,128)(2,1)S(1)}, u32[]{:S(2)}, u32[]{:S(2)}) %all-to-all-start.1) | async-done | bytes 884768 | tf_op jit(solution)/shard_map/all_to_all | solution.py:75
  76.6 2.0 bitcast_add_fusion.1
  79.5 1.6 multiply_convert_fusion.5
  81.9 1.4 select_bitcast_fusion.1
  83.3 3.8 %collective-permute-done.8 = bf16[128,576]{0,1:T(8,128)(2,1)S(1)} collective-permute-done((bf16[128,576]{0,1:T(8,128)(2,1)S(1)}, bf16[128,576]{0,1:T(8,128)(2,1)S(1)}, u32[]{:S(2)}, u32[]{:S(2)}) %collective-permute-start.8) | collective-permute-done | bytes 147488 | tf_op jit(solution)/shard_map/ppermute | solution.py:53
  88.2 1.4 collective-permute-start.10
  91.2 2.5 collective-permute-done.11
  93.7 6.5 %collective-permute-done.10 = bf16[128,576]{0,1:T(8,128)(2,1)S(1)} collective-permute-done((bf16[128,576]{0,1:T(8,128)(2,1)S(1)}, bf16[128,576]{0,1:T(8,128)(2,1)S(1)}, u32[]{:S(2)}, u32[]{:S(2)}) %collective-permute-start.10) | collective-permute-done | bytes 147488 | tf_op jit(solution)/shard_map/ppermute | solution.py:53
  100.2 1.4 fusion.98
  104.1 3.9 %fusion.162 = (f32[3,3,128]{2,1,0:T(4,128)}, f32[3,3,128,512]{2,3,1,0:T(8,128)}) fusion(pred[128,512]{0,1:T(8,128)(4,1)} %copy-done.92, bf16[512,3,32]{0,2,1:T(8,128)(2,1)} %get-tuple-element.103, bf16[512,3,32]{0,2,1:T(8,128)(2,1)} %get-tuple-element.102, bf16[128,3,3,32]{0,3,2,1:T(8,128)(2,1)} %bitcast.528, bf16[128,3,3,32]{0,3,2,1:T(8,128)(2,1)} %bitcast.524), kind=kOutput, calls=%fused_computation.348 | convolution fusion | flops 78545408 | bytes 2773504 | tf_op jit(solution)/shard_map/sub | solution.py:208
  107.9 3.0 convolution_convert_fusion.6
  110.9 1.7 copy.97
  112.6 1.8 multiply_reduce_fusion.6
  117.2 1.5 collective-permute-start.13
  119.3 2.0 bitcast_add_fusion
  122.3 1.4 fusion.102
  123.7 1.5 fusion.146
  125.2 1.8 multiply_convert_fusion.3
  128.3 1.4 convolution_convert_fusion.4
  129.7 1.4 convolution_convert_fusion.5
  132.5 12.4 %convolution_bitcast_fusion.2 = f32[256,576]{0,1:T(8,128)S(1)} fusion(bf16[256,2,384]{2,0,1:T(8,128)(2,1)S(1)} %get-tuple-element.78, bf16[2,576,384]{2,1,0:T(8,128)(2,1)S(1)} %bitcast.471), kind=kOutput, calls=%fused_computation.72 | convolution fusion | flops 226492416 | bytes 1867776 | tf_op jit(solution)/shard_map/tbf,bdf->td/dot_general | solution.py:22
  147.5 3.5 %collective-permute-done.16 = bf16[128,576]{0,1:T(8,128)(2,1)S(1)} collective-permute-done((bf16[128,576]{0,1:T(8,128)(2,1)S(1)}, bf16[128,576]{0,1:T(8,128)(2,1)S(1)}, u32[]{:S(2)}, u32[]{:S(2)}) %collective-permute-start.16) | collective-permute-done | bytes 147488 | tf_op jit(solution)/shard_map/ppermute | solution.py:53
  151.8 2.3 collective-permute-done.14
  159.1 3.0 fusion.48
  162.0 2.5 fusion.7
  167.9 2.3 copy.105
  170.1 3.4 %fusion.163 = (bf16[512,576]{0,1:T(8,128)(2,1)S(1)}, f32[512,576]{0,1:T(8,128)}) fusion(bf16[4,576,384]{2,1,0:T(8,128)(2,1)S(1)} %bitcast.463, bf16[512,4,240]{2,0,1:T(8,128)(2,1)} %copy.105), kind=kOutput, calls=%fused_computation.349 | convolution fusion | flops 906264576 | bytes 4521984 | tf_op jit(solution)/shard_map/trk,rdk->td/dot_general | solution.py:22
  176.3 2.8 collective-permute-done.20
  179.2 4.3 %collective-permute-done.19 = bf16[128,576]{0,1:T(8,128)(2,1)S(1)} collective-permute-done((bf16[128,576]{0,1:T(8,128)(2,1)S(1)}, bf16[128,576]{0,1:T(8,128)(2,1)S(1)}, u32[]{:S(2)}, u32[]{:S(2)}) %collective-permute-start.19) | collective-permute-done | bytes 147488 | tf_op jit(solution)/shard_map/ppermute | solution.py:53
  183.5 1.9 multiply_reduce_fusion.1
  187.3 2.4 fusion.64
  198.0 7.5 %collective-permute-done.36 = bf16[3,4,72,384]{3,2,0,1:T(8,128)(2,1)S(1)} collective-permute-done((bf16[3,4,72,384]{3,2,0,1:T(8,128)(2,1)S(1)}, bf16[3,4,72,384]{3,2,0,1:T(8,128)(2,1)S(1)}, u32[]{:S(2)}, u32[]{:S(2)}) %collective-permute-start.36) | collective-permute-done | bytes 663584 | tf_op jit(solution)/shard_map/ppermute | solution.py:53
  208.4 3.5 %add_convert_fusion = bf16[4,384,576]{1,2,0:T(8,128)(2,1)S(1)} fusion(f32[4,384,576]{1,2,0:T(8,128)} %fusion.64, f32[]{:T(128)} %bitcast.171, bf16[512,4,240]{2,0,1:T(8,128)(2,1)} %copy.105, bf16[128,576]{0,1:T(8,128)(2,1)S(1)} %copy-done.109, bf16[128,576]{0,1:T(8,128)(2,1)S(1)} %copy-done.111, bf16[128,576]{0,1:T(8,128)(2,1)} %copy-done.112, ...), kind=kOutput, calls=%fused_computation.2 | convolution fusion | flops 910983168 | bytes 6881284 | tf_op jit(solution)/shard_map/td,trk->rdk/dot_general | solution.py:22
  213.0 1.7 collective-permute-start.37
  219.1 1.8 collective-permute-done.22
  222.7 1.9 multiply_add_fusion
  224.6 2.6 fusion.14
  227.2 4.3 %all-to-all-start.2 = ((bf16[16,72,384]{2,1,0:T(8,128)(2,1)}), bf16[16,72,384]{2,1,0:T(8,128)(2,1)}, u32[]{:S(2)}, u32[]{:S(2)}) async-start(bf16[16,72,384]{2,1,0:T(8,128)(2,1)} %bitcast.479), calls=%async_computation.2 | async-start | bytes 1769472 | tf_op jit(solution)/shard_map/all_to_all | solution.py:97
  231.6 1.7 fusion.2
  241.0 2.7 fusion.49
  244.8 1.5 copy.112
  246.4 4.4 %fusion.16 = f32[4,384,576]{1,2,0:T(8,128)} fusion(bf16[512,4,240]{2,0,1:T(8,128)(2,1)} %copy.112, f32[576]{0:T(1024)S(1)} %copy-done.95, f32[512]{0:T(512)S(1)} %copy-done.107, bf16[128,576]{0,1:T(8,128)(2,1)S(1)} %copy-done.79, bf16[128,576]{0,1:T(8,128)(2,1)S(1)} %copy-done.76, bf16[128,576]{0,1:T(8,128)(2,1)S(1)} %copy-done.73, ...), kind=kOutput, calls=%fused_computation.43 | convolution fusion | flops 909213696 | bytes 5116160 | tf_op jit(solution)/shard_map/td,trk->rdk/dot_general | solution.py:22
  250.7 7.4 %collective-permute-done.27 = bf16[3,4,72,384]{3,2,0,1:T(8,128)(2,1)} collective-permute-done((bf16[3,4,72,384]{3,2,0,1:T(8,128)(2,1)}, bf16[3,4,72,384]{3,2,0,1:T(8,128)(2,1)}, u32[]{:S(2)}, u32[]{:S(2)}) %collective-permute-start.27) | collective-permute-done | bytes 663584 | tf_op jit(solution)/shard_map/ppermute | solution.py:53
  260.7 2.8 add_convert_fusion.1
  264.6 2.3 collective-permute-start.28
  266.9 2.2 fusion.40
  270.6 3.8 %collective-permute-start.26 = (bf16[128,576]{0,1:T(8,128)(2,1)}, bf16[128,576]{0,1:T(8,128)(2,1)S(1)}, u32[]{:S(2)}, u32[]{:S(2)}) collective-permute-start(bf16[128,576]{0,1:T(8,128)(2,1)} %get-tuple-element.93), channel_id=1, source_target_pairs={{0,12},{4,8},{8,4},{12,0},{1,13},{5,9},{9,5},{13,1},{2,14},{6,10},... | collective-permute-start | bytes 442376 | tf_op jit(solution)/shard_map/ppermute | solution.py:53
  275.3 1.5 fusion.15
  276.9 2.0 collective-permute-start.32
  280.5 2.0 collective-permute-done.25
  285.1 1.8 collective-permute-done.32
  286.9 5.8 %collective-permute-done.31 = bf16[4,80,384]{2,1,0:T(8,128)(2,1)S(1)} collective-permute-done((bf16[4,80,384]{2,1,0:T(8,128)(2,1)S(1)}, bf16[4,80,384]{2,1,0:T(8,128)(2,1)S(1)}, u32[]{:S(2)}, u32[]{:S(2)}) %collective-permute-start.31) | collective-permute-done | bytes 245792 | tf_op jit(solution)/shard_map/ppermute | solution.py:53
  292.8 4.7 %collective-permute-start.35 = (bf16[80,384]{1,0:T(8,128)(2,1)S(1)}, bf16[80,384]{1,0:T(8,128)(2,1)S(1)}, u32[]{:S(2)}, u32[]{:S(2)}) collective-permute-start(bf16[80,384]{1,0:T(8,128)(2,1)S(1)} %get-tuple-element.121), channel_id=1, source_target_pairs={{0,3},{1,2},{2,1},{3,0},{4,7},{5,6},{6,5},{7,4},{8,11},{9,10},{10,... | collective-permute-start | bytes 184328 | tf_op jit(solution)/shard_map/ppermute | solution.py:53
  300.4 3.3 %collective-permute-done.34 = bf16[80,384]{1,0:T(8,128)(2,1)S(1)} collective-permute-done((bf16[80,384]{1,0:T(8,128)(2,1)S(1)}, bf16[80,384]{1,0:T(8,128)(2,1)S(1)}, u32[]{:S(2)}, u32[]{:S(2)}) %collective-permute-start.34) | collective-permute-done | bytes 61472 | tf_op jit(solution)/shard_map/ppermute | solution.py:53
  305.7 1.8 fusion.77
  (452 shorter events, 91.9 us)
Async XLA Ops:
  7.2 69.4 %all-gather.5.cloned.1.call-start = ((), (), s32[]{:S(2)}) async-start(), calls=%async_computation.5 | async-start | bytes 2820096 | tf_op jit(solution)/shard_map/all_gather | solution.py:92
  9.4 110.0 %all-gather.7.cloned.1.call-start = ((), (), s32[]{:S(2)}) async-start(), calls=%async_computation.6 | async-start | bytes 2820096 | tf_op jit(solution)/shard_map/all_gather | solution.py:92
  9.7 8.4 %collective-permute-start.5 = (bf16[2,72,384]{2,1,0:T(8,128)(2,1)S(1)}, bf16[2,72,384]{2,1,0:T(8,128)(2,1)S(1)}, u32[]{:S(2)}, u32[]{:S(2)}) collective-permute-start(bf16[2,72,384]{2,1,0:T(8,128)(2,1)S(1)} %fusion.107), channel_id=1, source_target_pairs={{0,3},{1,2},{2,1},{3,0},{4,7},{5,6},{6,5},{7,4},{8,11},{9,10},{10,... | collective-permute-start | bytes 331784 | tf_op jit(solution)/shard_map/ppermute | solution.py:53
  13.9 8.9 %collective-permute-start.4 = (bf16[2,72,384]{2,1,0:T(8,128)(2,1)S(1)}, bf16[2,72,384]{2,1,0:T(8,128)(2,1)S(1)}, u32[]{:S(2)}, u32[]{:S(2)}) collective-permute-start(bf16[2,72,384]{2,1,0:T(8,128)(2,1)S(1)} %fusion.107), channel_id=1, source_target_pairs={{0,2},{1,3},{2,0},{3,1},{4,6},{5,7},{6,4},{7,5},{8,10},{9,11},{10,... | collective-permute-start | bytes 331784 | tf_op jit(solution)/shard_map/ppermute | solution.py:53
  13.9 8.9 %collective-permute-start.3 = (bf16[2,72,384]{2,1,0:T(8,128)(2,1)S(1)}, bf16[2,72,384]{2,1,0:T(8,128)(2,1)S(1)}, u32[]{:S(2)}, u32[]{:S(2)}) collective-permute-start(bf16[2,72,384]{2,1,0:T(8,128)(2,1)S(1)} %fusion.107), channel_id=1, source_target_pairs={{0,1},{1,0},{2,3},{3,2},{4,5},{5,4},{6,7},{7,6},{8,9},{9,8},{10,11... | collective-permute-start | bytes 331784 | tf_op jit(solution)/shard_map/ppermute | solution.py:53
  14.3 8.8 %collective-permute-start = (bf16[128,576]{0,1:T(8,128)(2,1)S(1)}, bf16[128,576]{0,1:T(8,128)(2,1)S(1)}, u32[]{:S(2)}, u32[]{:S(2)}) collective-permute-start(bf16[128,576]{0,1:T(8,128)(2,1)S(1)} %copy-done.31), channel_id=1, source_target_pairs={{0,4},{4,0},{8,12},{12,8},{1,5},{5,1},{9,13},{13,9},{2,6},{6,2},{1... | collective-permute-start | bytes 442376 | tf_op jit(solution)/shard_map/ppermute | solution.py:53
  15.5 8.8 %collective-permute-start.1 = (bf16[128,576]{0,1:T(8,128)(2,1)S(1)}, bf16[128,576]{0,1:T(8,128)(2,1)S(1)}, u32[]{:S(2)}, u32[]{:S(2)}) collective-permute-start(bf16[128,576]{0,1:T(8,128)(2,1)S(1)} %copy-done.31), channel_id=1, source_target_pairs={{0,8},{4,12},{8,0},{12,4},{1,9},{5,13},{9,1},{13,5},{2,10},{6,14},... | collective-permute-start | bytes 442376 | tf_op jit(solution)/shard_map/ppermute | solution.py:53
  18.1 7.4 %collective-permute-start.2 = (bf16[128,576]{0,1:T(8,128)(2,1)S(1)}, bf16[128,576]{0,1:T(8,128)(2,1)S(1)}, u32[]{:S(2)}, u32[]{:S(2)}) collective-permute-start(bf16[128,576]{0,1:T(8,128)(2,1)S(1)} %copy-done.31), channel_id=1, source_target_pairs={{0,12},{4,8},{8,4},{12,0},{1,13},{5,9},{9,5},{13,1},{2,14},{6,10},... | collective-permute-start | bytes 442376 | tf_op jit(solution)/shard_map/ppermute | solution.py:53
  23.1 25.8 %copy-start.72 = (bf16[128,576]{0,1:T(8,128)(2,1)}, bf16[128,576]{0,1:T(8,128)(2,1)S(1)}, u32[]{:S(2)}) copy-start(bf16[128,576]{0,1:T(8,128)(2,1)S(1)} %collective-permute-done) | copy-start | bytes 442372
  24.3 24.6 %copy-start.75 = (bf16[128,576]{0,1:T(8,128)(2,1)}, bf16[128,576]{0,1:T(8,128)(2,1)S(1)}, u32[]{:S(2)}) copy-start(bf16[128,576]{0,1:T(8,128)(2,1)S(1)} %collective-permute-done.1) | copy-start | bytes 442372
  25.5 23.3 %copy-start.78 = (bf16[128,576]{0,1:T(8,128)(2,1)}, bf16[128,576]{0,1:T(8,128)(2,1)S(1)}, u32[]{:S(2)}) copy-start(bf16[128,576]{0,1:T(8,128)(2,1)S(1)} %collective-permute-done.2) | copy-start | bytes 442372
  26.8 19.7 %copy-start.97 = (f32[2,2,576]{2,1,0:T(2,128)S(1)}, f32[2,2,576]{2,1,0:T(2,128)}, u32[]{:S(2)}) copy-start(f32[2,2,576]{2,1,0:T(2,128)} %param.12) | copy-start | bytes 27652
  27.8 15.1 %all-to-all-start = ((bf16[4,4,72,384]{3,2,1,0:T(8,128)(2,1)}), bf16[4,4,72,384]{3,2,1,0:T(8,128)(2,1)S(1)}, u32[]{:S(2)}, u32[]{:S(2)}) async-start(bf16[4,4,72,384]{3,2,1,0:T(8,128)(2,1)} %broadcast_in_dim.20), calls=%async_computation | async-start | bytes 1769472 | tf_op jit(solution)/shard_map/all_to_all | solution.py:75
  32.3 18.8 %copy-start.35 = (f32[512,32]{0,1:T(8,128)}, f32[512,32]{0,1:T(8,128)S(1)}, u32[]{:S(2)}) copy-start(f32[512,32]{0,1:T(8,128)S(1)} %get-tuple-element.127) | copy-start | bytes 196612
  32.3 18.9 %copy-start.49 = (f32[512,32]{0,1:T(8,128)}, f32[512,32]{0,1:T(8,128)S(1)}, u32[]{:S(2)}) copy-start(f32[512,32]{0,1:T(8,128)S(1)} %get-tuple-element.126) | copy-start | bytes 196612
  42.9 5.5 %collective-permute-start.6 = (bf16[4,4,72,384]{3,2,1,0:T(8,128)(2,1)S(1)}, bf16[4,4,72,384]{3,2,1,0:T(8,128)(2,1)S(1)}, u32[]{:S(2)}, u32[]{:S(2)}) collective-permute-start(bf16[4,4,72,384]{3,2,1,0:T(8,128)(2,1)S(1)} %all-to-all-done), channel_id=1, source_target_pairs={{0,16},{16,0},{1,17},{17,1},{2,18},{18,2},{3,19},{19,3},{4,20},{20... | collective-permute-start | bytes 2654216 | tf_op jit(solution)/shard_map/ppermute | solution.py:53
  47.1 14.3 %copy-start.87 = (f32[576]{0:T(1024)}, f32[576]{0:T(1024)S(1)}, u32[]{:S(2)}) copy-start(f32[576]{0:T(1024)S(1)} %get-tuple-element.47) | copy-start | bytes 6916
  47.1 40.2 %copy-start.88 = (f32[576]{0:T(1024)}, f32[576]{0:T(1024)S(1)}, u32[]{:S(2)}) copy-start(f32[576]{0:T(1024)S(1)} %get-tuple-element.49) | copy-start | bytes 6916
  55.8 31.3 %copy-start.2 = (f32[128,576]{0,1:T(8,128)}, f32[128,576]{0,1:T(8,128)S(1)}, u32[]{:S(2)}) copy-start(f32[128,576]{0,1:T(8,128)S(1)} %get-tuple-element.131) | copy-start | bytes 884740
  57.6 16.8 %all-to-all-start.1 = ((bf16[4,4,72,384]{3,2,1,0:T(8,128)(2,1)}), bf16[4,4,72,384]{3,2,1,0:T(8,128)(2,1)S(1)}, u32[]{:S(2)}, u32[]{:S(2)}) async-start(bf16[4,4,72,384]{3,2,1,0:T(8,128)(2,1)} %broadcast_in_dim.23), calls=%async_computation.1 | async-start | bytes 1769472 | tf_op jit(solution)/shard_map/all_to_all | solution.py:75
  61.1 236.8 %reduce-scatter.9.cloned.1.call-start = ((), (), s32[]{:S(2)}) async-start(), calls=%async_computation.8 | async-start | bytes 829440
  61.4 17.2 %copy-start.103 = (f32[128]{0:T(128)}, f32[128]{0:T(128)S(1)}, u32[]{:S(2)}) copy-start(f32[128]{0:T(128)S(1)} %add_rsqrt_fusion.3) | copy-start | bytes 1540
  61.6 17.9 %copy-start.27 = (bf16[128,576]{0,1:T(8,128)(2,1)}, bf16[128,576]{0,1:T(8,128)(2,1)S(1)}, u32[]{:S(2)}) copy-start(bf16[128,576]{0,1:T(8,128)(2,1)S(1)} %multiply_convert_fusion.8) | copy-start | bytes 442372
  62.1 16.8 %collective-permute-start.7 = (bf16[128,576]{0,1:T(8,128)(2,1)S(1)}, bf16[128,576]{0,1:T(8,128)(2,1)S(1)}, u32[]{:S(2)}, u32[]{:S(2)}) collective-permute-start(bf16[128,576]{0,1:T(8,128)(2,1)S(1)} %multiply_convert_fusion.8), channel_id=1, source_target_pairs={{0,4},{4,0},{8,12},{12,8},{1,5},{5,1},{9,13},{13,9},{2,6},{6,2},{1... | collective-permute-start | bytes 442376 | tf_op jit(solution)/shard_map/ppermute | solution.py:53
  64.9 56.8 %collective-permute-start.15 = (bf16[128,576]{0,1:T(8,128)(2,1)}, bf16[128,576]{0,1:T(8,128)(2,1)}, u32[]{:S(2)}, u32[]{:S(2)}) collective-permute-start(bf16[128,576]{0,1:T(8,128)(2,1)} %broadcast_add_fusion.1), channel_id=1, source_target_pairs={{0,4},{4,0},{8,12},{12,8},{1,5},{5,1},{9,13},{13,9},{2,6},{6,2},{1... | collective-permute-start | bytes 442376 | tf_op jit(solution)/shard_map/ppermute | solution.py:53
  75.4 6.5 %collective-permute-start.12 = (bf16[4,4,72,384]{3,2,1,0:T(8,128)(2,1)}, bf16[4,4,72,384]{3,2,1,0:T(8,128)(2,1)}, u32[]{:S(2)}, u32[]{:S(2)}) collective-permute-start(bf16[4,4,72,384]{3,2,1,0:T(8,128)(2,1)} %broadcast_add_fusion), channel_id=1, source_target_pairs={{0,16},{16,0},{1,17},{17,1},{2,18},{18,2},{3,19},{19,3},{4,20},{20... | collective-permute-start | bytes 2654216 | tf_op jit(solution)/shard_map/ppermute | solution.py:53
  81.6 5.5 %collective-permute-start.8 = (bf16[128,576]{0,1:T(8,128)(2,1)S(1)}, bf16[128,576]{0,1:T(8,128)(2,1)S(1)}, u32[]{:S(2)}, u32[]{:S(2)}) collective-permute-start(bf16[128,576]{0,1:T(8,128)(2,1)S(1)} %slice.502), channel_id=1, source_target_pairs={{0,4},{4,0},{8,12},{12,8},{1,5},{5,1},{9,13},{13,9},{2,6},{6,2},{1... | collective-permute-start | bytes 442376 | tf_op jit(solution)/shard_map/ppermute | solution.py:53
  88.1 12.1 %copy-start.81 = (bf16[128,576]{0,1:T(8,128)(2,1)}, bf16[128,576]{0,1:T(8,128)(2,1)S(1)}, u32[]{:S(2)}) copy-start(bf16[128,576]{0,1:T(8,128)(2,1)S(1)} %multiply_convert_fusion.7) | copy-start | bytes 442372
  88.1 5.6 %collective-permute-start.11 = (bf16[128,576]{0,1:T(8,128)(2,1)S(1)}, bf16[128,576]{0,1:T(8,128)(2,1)S(1)}, u32[]{:S(2)}, u32[]{:S(2)}) collective-permute-start(bf16[128,576]{0,1:T(8,128)(2,1)S(1)} %multiply_convert_fusion.7), channel_id=1, source_target_pairs={{0,12},{4,8},{8,4},{12,0},{1,13},{5,9},{9,5},{13,1},{2,14},{6,10},... | collective-permute-start | bytes 442376 | tf_op jit(solution)/shard_map/ppermute | solution.py:53
  88.2 12.0 %collective-permute-start.10 = (bf16[128,576]{0,1:T(8,128)(2,1)S(1)}, bf16[128,576]{0,1:T(8,128)(2,1)S(1)}, u32[]{:S(2)}, u32[]{:S(2)}) collective-permute-start(bf16[128,576]{0,1:T(8,128)(2,1)S(1)} %multiply_convert_fusion.7), channel_id=1, source_target_pairs={{0,8},{4,12},{8,0},{12,4},{1,9},{5,13},{9,1},{13,5},{2,10},{6,14},... | collective-permute-start | bytes 442376 | tf_op jit(solution)/shard_map/ppermute | solution.py:53
  89.6 10.5 %collective-permute-start.9 = (bf16[128,576]{0,1:T(8,128)(2,1)S(1)}, bf16[128,576]{0,1:T(8,128)(2,1)S(1)}, u32[]{:S(2)}, u32[]{:S(2)}) collective-permute-start(bf16[128,576]{0,1:T(8,128)(2,1)S(1)} %multiply_convert_fusion.7), channel_id=1, source_target_pairs={{0,4},{4,0},{8,12},{12,8},{1,5},{5,1},{9,13},{13,9},{2,6},{6,2},{1... | collective-permute-start | bytes 442376 | tf_op jit(solution)/shard_map/ppermute | solution.py:53
  117.2 6.5 %collective-permute-start.13 = (bf16[128,576]{0,1:T(8,128)(2,1)}, bf16[128,576]{0,1:T(8,128)(2,1)}, u32[]{:S(2)}, u32[]{:S(2)}) collective-permute-start(bf16[128,576]{0,1:T(8,128)(2,1)} %multiply_convert_fusion.6), channel_id=1, source_target_pairs={{0,4},{4,0},{8,12},{12,8},{1,5},{5,1},{9,13},{13,9},{2,6},{6,2},{1... | collective-permute-start | bytes 442376 | tf_op jit(solution)/shard_map/ppermute | solution.py:53
  131.9 23.0 %collective-permute-start.17 = (bf16[2,3,4,72,384]{4,3,1,2,0:T(8,128)(2,1)S(1)}, bf16[2,3,4,72,384]{4,3,1,2,0:T(8,128)(2,1)S(1)}, u32[]{:S(2)}, u32[]{:S(2)}) collective-permute-start(bf16[2,3,4,72,384]{4,3,1,2,0:T(8,128)(2,1)S(1)} %bitcast.502), channel_id=1, source_target_pairs={{0,16},{16,0},{1,17},{17,1},{2,18},{18,2},{3,19},{19,3},{4,20},{20... | collective-permute-start | bytes 3981320 | tf_op jit(solution)/shard_map/ppermute | solution.py:53
  145.4 5.5 %collective-permute-start.16 = (bf16[128,576]{0,1:T(8,128)(2,1)S(1)}, bf16[128,576]{0,1:T(8,128)(2,1)S(1)}, u32[]{:S(2)}, u32[]{:S(2)}) collective-permute-start(bf16[128,576]{0,1:T(8,128)(2,1)S(1)} %slice.500), channel_id=1, source_target_pairs={{0,4},{4,0},{8,12},{12,8},{1,5},{5,1},{9,13},{13,9},{2,6},{6,2},{1... | collective-permute-start | bytes 442376 | tf_op jit(solution)/shard_map/ppermute | solution.py:53
  146.9 7.2 %collective-permute-start.14 = (bf16[128,576]{0,1:T(8,128)(2,1)S(1)}, bf16[128,576]{0,1:T(8,128)(2,1)S(1)}, u32[]{:S(2)}, u32[]{:S(2)}) collective-permute-start(bf16[128,576]{0,1:T(8,128)(2,1)S(1)} %slice.501), channel_id=1, source_target_pairs={{0,4},{4,0},{8,12},{12,8},{1,5},{5,1},{9,13},{13,9},{2,6},{6,2},{1... | collective-permute-start | bytes 442376 | tf_op jit(solution)/shard_map/ppermute | solution.py:53
  173.5 13.8 %copy-start.30 = (bf16[128,4,144]{2,0,1:T(8,128)(2,1)S(1)}, bf16[128,4,144]{2,0,1:T(8,128)(2,1)}, u32[]{:S(2)}) copy-start(bf16[128,4,144]{2,0,1:T(8,128)(2,1)} %copy.97) | copy-start | bytes 442372
  173.6 5.5 %collective-permute-start.20 = (bf16[128,576]{0,1:T(8,128)(2,1)S(1)}, bf16[128,576]{0,1:T(8,128)(2,1)S(1)}, u32[]{:S(2)}, u32[]{:S(2)}) collective-permute-start(bf16[128,576]{0,1:T(8,128)(2,1)S(1)} %get-tuple-element.96), channel_id=1, source_target_pairs={{0,12},{4,8},{8,4},{12,0},{1,13},{5,9},{9,5},{13,1},{2,14},{6,10},... | collective-permute-start | bytes 442376 | tf_op jit(solution)/shard_map/ppermute | solution.py:53
  174.8 8.7 %collective-permute-start.19 = (bf16[128,576]{0,1:T(8,128)(2,1)S(1)}, bf16[128,576]{0,1:T(8,128)(2,1)S(1)}, u32[]{:S(2)}, u32[]{:S(2)}) collective-permute-start(bf16[128,576]{0,1:T(8,128)(2,1)S(1)} %get-tuple-element.97), channel_id=1, source_target_pairs={{0,8},{4,12},{8,0},{12,4},{1,9},{5,13},{9,1},{13,5},{2,10},{6,14},... | collective-permute-start | bytes 442376 | tf_op jit(solution)/shard_map/ppermute | solution.py:53
  175.9 7.7 %collective-permute-start.18 = (bf16[128,576]{0,1:T(8,128)(2,1)S(1)}, bf16[128,576]{0,1:T(8,128)(2,1)S(1)}, u32[]{:S(2)}, u32[]{:S(2)}) collective-permute-start(bf16[128,576]{0,1:T(8,128)(2,1)S(1)} %get-tuple-element.95), channel_id=1, source_target_pairs={{0,4},{4,0},{8,12},{12,8},{1,5},{5,1},{9,13},{13,9},{2,6},{6,2},{1... | collective-permute-start | bytes 442376 | tf_op jit(solution)/shard_map/ppermute | solution.py:53
  186.3 4.9 %collective-permute-start.21 = (bf16[128,576]{0,1:T(8,128)(2,1)S(1)}, bf16[128,576]{0,1:T(8,128)(2,1)S(1)}, u32[]{:S(2)}, u32[]{:S(2)}) collective-permute-start(bf16[128,576]{0,1:T(8,128)(2,1)S(1)} %get-tuple-element.50), channel_id=1, source_target_pairs={{0,4},{4,0},{8,12},{12,8},{1,5},{5,1},{9,13},{13,9},{2,6},{6,2},{1... | collective-permute-start | bytes 442376 | tf_op jit(solution)/shard_map/ppermute | solution.py:53
  189.8 15.7 %collective-permute-start.36 = (bf16[3,4,72,384]{3,2,0,1:T(8,128)(2,1)S(1)}, bf16[3,4,72,384]{3,2,0,1:T(8,128)(2,1)S(1)}, u32[]{:S(2)}, u32[]{:S(2)}) collective-permute-start(bf16[3,4,72,384]{3,2,0,1:T(8,128)(2,1)S(1)} %dynamic-slice_bitcast_fusion.2), channel_id=1, source_target_pairs={{0,8},{4,12},{8,0},{12,4},{1,9},{5,13},{9,1},{13,5},{2,10},{6,14},... | collective-permute-start | bytes 1990664 | tf_op jit(solution)/shard_map/ppermute | solution.py:53
  195.4 13.0 %copy-start.82 = (bf16[128,576]{0,1:T(8,128)(2,1)S(1)}, bf16[128,576]{0,1:T(8,128)(2,1)}, u32[]{:S(2)}) copy-start(bf16[128,576]{0,1:T(8,128)(2,1)} %copy-done.81) | copy-start | bytes 442372
  195.4 13.0 %copy-start.109 = (bf16[128,576]{0,1:T(8,128)(2,1)S(1)}, bf16[128,576]{0,1:T(8,128)(2,1)}, u32[]{:S(2)}) copy-start(bf16[128,576]{0,1:T(8,128)(2,1)} %copy-done.108) | copy-start | bytes 442372
  195.4 13.0 %copy-start.111 = (bf16[128,576]{0,1:T(8,128)(2,1)S(1)}, bf16[128,576]{0,1:T(8,128)(2,1)}, u32[]{:S(2)}) copy-start(bf16[128,576]{0,1:T(8,128)(2,1)} %copy-done.110) | copy-start | bytes 442372
  195.4 36.2 %collective-permute-start.23 = (bf16[2,3,4,72,384]{4,3,1,2,0:T(8,128)(2,1)}, bf16[2,3,4,72,384]{4,3,1,2,0:T(8,128)(2,1)}, u32[]{:S(2)}, u32[]{:S(2)}) collective-permute-start(bf16[2,3,4,72,384]{4,3,1,2,0:T(8,128)(2,1)} %bitcast.452), channel_id=1, source_target_pairs={{0,16},{16,0},{1,17},{17,1},{2,18},{18,2},{3,19},{19,3},{4,20},{20... | collective-permute-start | bytes 3981320 | tf_op jit(solution)/shard_map/ppermute | solution.py:53
  213.0 11.7 %collective-permute-start.37 = (bf16[4,4,72,384]{3,2,1,0:T(8,128)(2,1)}, bf16[4,4,72,384]{3,2,1,0:T(8,128)(2,1)}, u32[]{:S(2)}, u32[]{:S(2)}) collective-permute-start(bf16[4,4,72,384]{3,2,1,0:T(8,128)(2,1)} %dynamic-slice_bitcast_fusion), channel_id=1, source_target_pairs={{0,16},{16,0},{1,17},{17,1},{2,18},{18,2},{3,19},{19,3},{4,20},{20... | collective-permute-start | bytes 2654216 | tf_op jit(solution)/shard_map/ppermute | solution.py:53
  216.7 4.2 %collective-permute-start.22 = (bf16[128,576]{0,1:T(8,128)(2,1)}, bf16[128,576]{0,1:T(8,128)(2,1)S(1)}, u32[]{:S(2)}, u32[]{:S(2)}) collective-permute-start(bf16[128,576]{0,1:T(8,128)(2,1)} %slice.498), channel_id=1, source_target_pairs={{0,4},{4,0},{8,12},{12,8},{1,5},{5,1},{9,13},{13,9},{2,6},{6,2},{1... | collective-permute-start | bytes 442376 | tf_op jit(solution)/shard_map/ppermute | solution.py:53
  227.2 56.5 %all-to-all-start.2 = ((bf16[16,72,384]{2,1,0:T(8,128)(2,1)}), bf16[16,72,384]{2,1,0:T(8,128)(2,1)}, u32[]{:S(2)}, u32[]{:S(2)}) async-start(bf16[16,72,384]{2,1,0:T(8,128)(2,1)} %bitcast.479), calls=%async_computation.2 | async-start | bytes 1769472 | tf_op jit(solution)/shard_map/all_to_all | solution.py:97
  231.5 72.3 %reduce-scatter.7.cloned.1.call-start = ((), (), s32[]{:S(2)}) async-start(), calls=%async_computation.7 | async-start | bytes 829440
  239.6 18.5 %collective-permute-start.27 = (bf16[3,4,72,384]{3,2,0,1:T(8,128)(2,1)}, bf16[3,4,72,384]{3,2,0,1:T(8,128)(2,1)}, u32[]{:S(2)}, u32[]{:S(2)}) collective-permute-start(bf16[3,4,72,384]{3,2,0,1:T(8,128)(2,1)} %dynamic-slice_bitcast_fusion.3), channel_id=1, source_target_pairs={{0,8},{4,12},{8,0},{12,4},{1,9},{5,13},{9,1},{13,5},{2,10},{6,14},... | collective-permute-start | bytes 1990664 | tf_op jit(solution)/shard_map/ppermute | solution.py:53
  264.6 10.7 %collective-permute-start.28 = (bf16[4,4,72,384]{3,2,1,0:T(8,128)(2,1)}, bf16[4,4,72,384]{3,2,1,0:T(8,128)(2,1)}, u32[]{:S(2)}, u32[]{:S(2)}) collective-permute-start(bf16[4,4,72,384]{3,2,1,0:T(8,128)(2,1)} %dynamic-slice_bitcast_fusion.1), channel_id=1, source_target_pairs={{0,16},{16,0},{1,17},{17,1},{2,18},{18,2},{3,19},{19,3},{4,20},{20... | collective-permute-start | bytes 2654216 | tf_op jit(solution)/shard_map/ppermute | solution.py:53
  269.1 6.0 %collective-permute-start.29 = (f32[2,2,576]{2,1,0:T(2,128)S(1)}, f32[2,2,576]{2,1,0:T(2,128)S(1)}, u32[]{:S(2)}, u32[]{:S(2)}) collective-permute-start(f32[2,2,576]{2,1,0:T(2,128)S(1)} %pad_maximum_fusion.22), channel_id=1, source_target_pairs={{0,16},{16,0},{1,17},{17,1},{2,18},{18,2},{3,19},{19,3},{4,20},{20... | collective-permute-start | bytes 27656 | tf_op jit(solution)/shard_map/ppermute | solution.py:53
  270.6 9.0 %collective-permute-start.26 = (bf16[128,576]{0,1:T(8,128)(2,1)}, bf16[128,576]{0,1:T(8,128)(2,1)S(1)}, u32[]{:S(2)}, u32[]{:S(2)}) collective-permute-start(bf16[128,576]{0,1:T(8,128)(2,1)} %get-tuple-element.93), channel_id=1, source_target_pairs={{0,12},{4,8},{8,4},{12,0},{1,13},{5,9},{9,5},{13,1},{2,14},{6,10},... | collective-permute-start | bytes 442376 | tf_op jit(solution)/shard_map/ppermute | solution.py:53
  274.4 8.2 %collective-permute-start.25 = (bf16[128,576]{0,1:T(8,128)(2,1)}, bf16[128,576]{0,1:T(8,128)(2,1)S(1)}, u32[]{:S(2)}, u32[]{:S(2)}) collective-permute-start(bf16[128,576]{0,1:T(8,128)(2,1)} %get-tuple-element.94), channel_id=1, source_target_pairs={{0,8},{4,12},{8,0},{12,4},{1,9},{5,13},{9,1},{13,5},{2,10},{6,14},... | collective-permute-start | bytes 442376 | tf_op jit(solution)/shard_map/ppermute | solution.py:53
  275.1 7.5 %collective-permute-start.24 = (bf16[128,576]{0,1:T(8,128)(2,1)}, bf16[128,576]{0,1:T(8,128)(2,1)S(1)}, u32[]{:S(2)}, u32[]{:S(2)}) collective-permute-start(bf16[128,576]{0,1:T(8,128)(2,1)} %get-tuple-element.92), channel_id=1, source_target_pairs={{0,4},{4,0},{8,12},{12,8},{1,5},{5,1},{9,13},{13,9},{2,6},{6,2},{1... | collective-permute-start | bytes 442376 | tf_op jit(solution)/shard_map/ppermute | solution.py:53
  276.9 10.0 %collective-permute-start.32 = (bf16[4,80,384]{2,1,0:T(8,128)(2,1)S(1)}, bf16[4,80,384]{2,1,0:T(8,128)(2,1)S(1)}, u32[]{:S(2)}, u32[]{:S(2)}) collective-permute-start(bf16[4,80,384]{2,1,0:T(8,128)(2,1)S(1)} %get-tuple-element.83), channel_id=1, source_target_pairs={{0,12},{4,8},{8,4},{12,0},{1,13},{5,9},{9,5},{13,1},{2,14},{6,10},... | collective-permute-start | bytes 737288 | tf_op jit(solution)/shard_map/ppermute | solution.py:53
  278.8 13.8 %collective-permute-start.31 = (bf16[4,80,384]{2,1,0:T(8,128)(2,1)S(1)}, bf16[4,80,384]{2,1,0:T(8,128)(2,1)S(1)}, u32[]{:S(2)}, u32[]{:S(2)}) collective-permute-start(bf16[4,80,384]{2,1,0:T(8,128)(2,1)S(1)} %get-tuple-element.82), channel_id=1, source_target_pairs={{0,8},{4,12},{8,0},{12,4},{1,9},{5,13},{9,1},{13,5},{2,10},{6,14},... | collective-permute-start | bytes 737288 | tf_op jit(solution)/shard_map/ppermute | solution.py:53
  279.6 13.0 %collective-permute-start.30 = (bf16[4,80,384]{2,1,0:T(8,128)(2,1)S(1)}, bf16[4,80,384]{2,1,0:T(8,128)(2,1)S(1)}, u32[]{:S(2)}, u32[]{:S(2)}) collective-permute-start(bf16[4,80,384]{2,1,0:T(8,128)(2,1)S(1)} %get-tuple-element.81), channel_id=1, source_target_pairs={{0,4},{4,0},{8,12},{12,8},{1,5},{5,1},{9,13},{13,9},{2,6},{6,2},{1... | collective-permute-start | bytes 737288 | tf_op jit(solution)/shard_map/ppermute | solution.py:53
  292.7 12.9 %copy-start.11 = (f32[128,576]{0,1:T(8,128)S(1)}, f32[128,576]{0,1:T(8,128)}, u32[]{:S(2)}) copy-start(f32[128,576]{0,1:T(8,128)} %multiply_add_fusion) | copy-start | bytes 884740
  292.8 12.9 %copy-start.52 = (bf16[128,576]{0,1:T(8,128)(2,1)S(1)}, bf16[128,576]{0,1:T(8,128)(2,1)}, u32[]{:S(2)}) copy-start(bf16[128,576]{0,1:T(8,128)(2,1)} %copy-done.51) | copy-start | bytes 442372
  292.8 7.6 %collective-permute-start.35 = (bf16[80,384]{1,0:T(8,128)(2,1)S(1)}, bf16[80,384]{1,0:T(8,128)(2,1)S(1)}, u32[]{:S(2)}, u32[]{:S(2)}) collective-permute-start(bf16[80,384]{1,0:T(8,128)(2,1)S(1)} %get-tuple-element.121), channel_id=1, source_target_pairs={{0,3},{1,2},{2,1},{3,0},{4,7},{5,6},{6,5},{7,4},{8,11},{9,10},{10,... | collective-permute-start | bytes 184328 | tf_op jit(solution)/shard_map/ppermute | solution.py:53
  297.5 6.2 %collective-permute-start.34 = (bf16[80,384]{1,0:T(8,128)(2,1)S(1)}, bf16[80,384]{1,0:T(8,128)(2,1)S(1)}, u32[]{:S(2)}, u32[]{:S(2)}) collective-permute-start(bf16[80,384]{1,0:T(8,128)(2,1)S(1)} %get-tuple-element.122), channel_id=1, source_target_pairs={{0,2},{1,3},{2,0},{3,1},{4,6},{5,7},{6,4},{7,5},{8,10},{9,11},{10,... | collective-permute-start | bytes 184328 | tf_op jit(solution)/shard_map/ppermute | solution.py:53
  297.5 6.2 %collective-permute-start.33 = (bf16[80,384]{1,0:T(8,128)(2,1)S(1)}, bf16[80,384]{1,0:T(8,128)(2,1)S(1)}, u32[]{:S(2)}, u32[]{:S(2)}) collective-permute-start(bf16[80,384]{1,0:T(8,128)(2,1)S(1)} %get-tuple-element.120), channel_id=1, source_target_pairs={{0,1},{1,0},{2,3},{3,2},{4,5},{5,4},{6,7},{7,6},{8,9},{9,8},{10,11... | collective-permute-start | bytes 184328 | tf_op jit(solution)/shard_map/ppermute | solution.py:53
  304.8 3.3 %collective-permute-start.38 = (bf16[2,4,72,384]{3,2,1,0:T(8,128)(2,1)S(1)}, bf16[2,4,72,384]{3,2,1,0:T(8,128)(2,1)S(1)}, u32[]{:S(2)}, u32[]{:S(2)}) collective-permute-start(bf16[2,4,72,384]{3,2,1,0:T(8,128)(2,1)S(1)} %maximum_add_fusion), channel_id=1, source_target_pairs={{0,16},{16,0},{1,17},{17,1},{2,18},{18,2},{3,19},{19,3},{4,20},{20... | collective-permute-start | bytes 1327112 | tf_op jit(solution)/shard_map/ppermute | solution.py:53
  (96 other events, 307.1 us)
Sparse Core Ops, SparseCore 0:
  10.8 47.4 all-gather.4
  60.5 49.8 all-gather.6
  224.8 29.6 reduce-scatter.8
  275.4 23.4 reduce-scatter.6
